TPU v7x, 512 devices: a whole 4x4x16 slice. The times are simulated.
512 devices in a mesh: batch: 8 (over z_lo, core), frame: 4 (over x), row: 16 (over z_hi, y).
Axes of the slice: x: 4, y: 4, z: 16 (z_hi: 4, z_lo: 4; z = z_hi * 4 + z_lo), core: 2. Of those that a mesh axis runs over, the one named last changes fastest.
Arguments:
- block_input: bfloat16 [8, 16, 128, 32, 128], P('batch', 'frame', 'row'), may hold values from -90 to 90
- gain_first: float32 [128], replicated, may hold values from 0.5 to 2
- conv_weight: bfloat16 [3, 3, 3, 128, 128], replicated, may hold values from -0.109375 to 0.109375
- gain_second: float32 [128], replicated, may hold values from 0.5 to 2
- out_weight: bfloat16 [128, 3], replicated, may hold values from -0.5 to 0.5
- disc_first: bfloat16 [1, 4, 4, 3, 64], replicated, may hold values from -0.875 to 0.875
- disc_second: bfloat16 [2, 4, 4, 64, 128], replicated, may hold values from -0.125 to 0.125
- score_grad: float32 [8, 8, 32, 8, 128], P('batch', 'frame', 'row'), may hold values from -800 to 800
Outputs:
- input_grad: bfloat16 [8, 16, 128, 32, 128], P('batch', 'frame', 'row')
- update: float32 [3, 3, 3, 128, 128], replicated
All inputs are finite; a program needn't handle non-finite values.
Results may differ from a plain program's by a relative error of at most 0.022.
Values may be sent and summed in bfloat16 or wider, within the bound.
A program may use at most 64 MiB of HBM per device.

v0:
```python
import jax
import jax.numpy as jnp
from jax import lax
from jax.sharding import PartitionSpec as P

GROUPS = 32


EPSILON = 1e-06


def with_halo(block, sides, width):
    for axis, dim in sides:
        count = lax.axis_size(axis)
        forward = [(i, i + 1) for i in range(count - 1)]
        backward = [(target, source) for source, target in forward]
        low = lax.ppermute(
            lax.slice_in_dim(block, block.shape[dim] - width, None, axis=dim), axis, forward
        )
        high = lax.ppermute(lax.slice_in_dim(block, 0, width, axis=dim), axis, backward)
        block = jnp.concatenate([low, block, high], axis=dim)
    return block


def passed_along(value, axis, steps):
    count = lax.axis_size(axis)
    leading, last = (max(0, -steps), min(count, count - steps))
    return lax.ppermute(value, axis, [(source, source + steps) for source in range(leading, last)])


def silu_slope(values):
    logistic = jax.nn.sigmoid(values)
    return logistic * (1.0 + values * (1.0 - logistic))


def group_sums(values, groups):
    shaped = values.reshape(values.shape[:-1] + (groups, values.shape[-1] // groups))
    return jnp.sum(shaped, axis=(0, 1, 2, 4))


def spread_channels(per_group, channel_count):
    return jnp.repeat(per_group, channel_count // per_group.shape[0])


def norm_forward(values, groups, member_count):
    channel_count = values.shape[-1]
    totals = lax.psum(group_sums(values, groups), ("frame", "row"))
    centred = values - spread_channels(totals / member_count, channel_count)
    variance = lax.psum(group_sums(centred * centred, groups), ("frame", "row")) / member_count
    inverse = spread_channels(lax.rsqrt(variance + EPSILON), channel_count)
    return (centred * inverse, inverse)


def norm_backward(act_grad, scaled, normed, inverse, gain, groups, member_count):
    channel_count = normed.shape[-1]
    weighted = act_grad * silu_slope(scaled) * gain
    first_sum, second_sum = lax.psum(
        (group_sums(weighted, groups), group_sums(weighted * normed, groups)), ("frame", "row")
    )
    first_mean = spread_channels(first_sum / member_count, channel_count)
    second_mean = spread_channels(second_sum / member_count, channel_count)
    return (weighted - first_mean - normed * second_mean) * inverse


def pad_columns(values):
    return jnp.pad(values, ((0, 0), (0, 0), (1, 1), (0, 0)))


def column_taps(window_slab, offsets, column_count):
    return jnp.concatenate(
        [
            lax.slice_in_dim(window_slab, offset, offset + column_count, axis=2)
            for offset in offsets
        ],
        axis=3,
    )


def causal_conv(extended, weight, frame_count, row_count, column_count):
    summed = None
    for tap_t in range(3):
        for tap_r in range(3):
            window_slab = extended[tap_t : tap_t + frame_count, tap_r : tap_r + row_count]
            stacked = column_taps(window_slab, (0, 1, 2), column_count)
            product_term = jnp.dot(
                stacked,
                weight[tap_t, tap_r].reshape(-1, weight.shape[-1]),
                preferred_element_type=jnp.float32,
            )
            summed = product_term if summed is None else summed + product_term
    return summed


def causal_conv_back(extended, weight, frame_count, row_count, column_count):
    flipped = jnp.swapaxes(weight, 3, 4)
    summed = None
    for tap_t in range(3):
        for tap_r in range(3):
            window_slab = extended[
                2 - tap_t : 2 - tap_t + frame_count, 2 - tap_r : 2 - tap_r + row_count
            ]
            stacked = column_taps(window_slab, (2, 1, 0), column_count)
            product_term = jnp.dot(
                stacked,
                flipped[tap_t, tap_r].reshape(-1, flipped.shape[-1]),
                preferred_element_type=jnp.float32,
            )
            summed = product_term if summed is None else summed + product_term
    return summed


def causal_conv_weight(extended, grad, frame_count, row_count, column_count):
    blocks = []
    for tap_t in range(3):
        for tap_r in range(3):
            window_slab = extended[tap_t : tap_t + frame_count, tap_r : tap_r + row_count]
            stacked = column_taps(window_slab, (0, 1, 2), column_count)
            blocks.append(
                lax.dot_general(
                    stacked,
                    grad,
                    (((0, 1, 2), (0, 1, 2)), ((), ())),
                    preferred_element_type=jnp.float32,
                )
            )
    channel_count = grad.shape[-1]
    return jnp.stack(blocks).reshape(3, 3, 3, channel_count, channel_count)


def strided_conv(extended, weight, rows_out):
    time_taps = weight.shape[0]
    cols_out = (extended.shape[2] - 2) // 2
    summed = None
    for tap_t in range(time_taps):
        for tap_r in range(4):
            for tap_c in range(4):
                source = extended[
                    tap_t::time_taps,
                    tap_r : tap_r + 2 * rows_out : 2,
                    tap_c : tap_c + 2 * cols_out : 2,
                ]
                product_term = jnp.dot(
                    source, weight[tap_t, tap_r, tap_c], preferred_element_type=jnp.float32
                )
                summed = product_term if summed is None else summed + product_term
    return summed


def strided_back(extended, weight):
    time_taps = weight.shape[0]
    frame_count, row_ext, col_ext, _ = extended.shape
    rows_out = row_ext - 2
    cols_out = col_ext - 2
    per_time = []
    for tap_t in range(time_taps):
        phases = [[None, None], [None, None]]
        for tap_r in range(4):
            for tap_c in range(4):
                row_start = 1 if tap_r < 2 else 0
                column_start = 1 if tap_c < 2 else 0
                source = extended[
                    :,
                    row_start : row_start + rows_out + 1,
                    column_start : column_start + cols_out + 1,
                ]
                product_term = jnp.dot(
                    source, weight[tap_t, tap_r, tap_c].T, preferred_element_type=jnp.float32
                )
                current = phases[tap_r % 2][tap_c % 2]
                phases[tap_r % 2][tap_c % 2] = (
                    product_term if current is None else current + product_term
                )
        upper = jnp.stack([phases[0][0], phases[0][1]], axis=3)
        lower = jnp.stack([phases[1][0], phases[1][1]], axis=3)
        grid = jnp.stack([upper, lower], axis=2)
        per_time.append(grid.reshape(frame_count, 2 * rows_out + 2, 2 * cols_out + 2, -1))
    joined = jnp.stack(per_time, axis=1)
    return joined.reshape((frame_count * time_taps,) + joined.shape[2:])


def shards(
    block_input,
    gain_first,
    conv_weight,
    gain_second,
    out_weight,
    disc_first,
    disc_second,
    score_grad,
):
    inputs = block_input[0]
    frame_count, row_count, column_count, channel_count = inputs.shape
    groups = GROUPS
    member_count = (
        frame_count
        * row_count
        * column_count
        * (channel_count // groups)
        * lax.axis_size("frame")
        * lax.axis_size("row")
    )
    wide_in = inputs.astype(jnp.float32)
    normed_first, inverse_first = norm_forward(wide_in, groups, member_count)
    scaled_first = normed_first * gain_first
    act_first = jax.nn.silu(scaled_first).astype(jnp.bfloat16)
    with_rows = with_halo(act_first, (("row", 1),), 1)
    earlier = passed_along(with_rows[frame_count - 2 :], "frame", 1)
    extended = pad_columns(jnp.concatenate([earlier, with_rows], axis=0))
    branch = causal_conv(extended, conv_weight, frame_count, row_count, column_count)
    mixed = (wide_in + branch).astype(jnp.bfloat16)
    normed_second, inverse_second = norm_forward(mixed.astype(jnp.float32), groups, member_count)
    scaled_second = normed_second * gain_second
    act_second = jax.nn.silu(scaled_second).astype(jnp.bfloat16)
    image = jnp.dot(act_second, out_weight, preferred_element_type=jnp.float32).astype(jnp.bfloat16)
    half_rows = row_count // 2
    image_ext = with_halo(image, (("row", 1),), 1)
    first_pre = strided_conv(pad_columns(image_ext), disc_first, half_rows)
    first_act = jax.nn.silu(first_pre).astype(jnp.bfloat16)
    first_ext = with_halo(first_act, (("row", 1),), 1)
    second_pre = strided_conv(pad_columns(first_ext), disc_second, row_count // 4)
    score_pre = (score_grad[0] * silu_slope(second_pre)).astype(jnp.bfloat16)
    score_ext = pad_columns(with_halo(score_pre, (("row", 1),), 1))
    first_full = strided_back(score_ext, disc_second)[:, :, 1:-1]
    first_grad = (first_full[:, 1:-1] * silu_slope(first_pre)).astype(jnp.bfloat16)
    feature_ext = with_halo(first_grad, (("row", 1),), 1)
    image_grad = strided_back(pad_columns(feature_ext), disc_first)[:, 1:-1, 1:-1].astype(
        jnp.bfloat16
    )
    act_grad = jnp.dot(image_grad, out_weight.T, preferred_element_type=jnp.float32)
    mixed_grad = norm_backward(
        act_grad, scaled_second, normed_second, inverse_second, gain_second, groups, member_count
    )
    branch_grad = mixed_grad.astype(jnp.bfloat16)
    grad_rows = with_halo(branch_grad, (("row", 1),), 1)
    later = passed_along(grad_rows[:2], "frame", -1)
    branch_ext = pad_columns(jnp.concatenate([grad_rows, later], axis=0))
    act_first_grad = causal_conv_back(branch_ext, conv_weight, frame_count, row_count, column_count)
    local_weight = causal_conv_weight(
        extended, branch_grad, frame_count, row_count, column_count
    ).reshape(-1)
    input_grad = (
        mixed_grad
        + norm_backward(
            act_first_grad,
            scaled_first,
            normed_first,
            inverse_first,
            gain_first,
            groups,
            member_count,
        )
    ).astype(jnp.bfloat16)
    summed_weight = lax.psum(local_weight, ("batch", "frame", "row"))
    update = summed_weight * lax.rsqrt(jnp.mean(summed_weight * summed_weight) + EPSILON)
    return (input_grad[None], update.reshape(conv_weight.shape))


def solution(mesh):
    in_specs = (
        P("batch", "frame", "row", None, None),
        P(),
        P(),
        P(),
        P(),
        P(),
        P(),
        P("batch", "frame", "row", None, None),
    )
    out_specs = (P("batch", "frame", "row", None, None), P())
    return jax.shard_map(shards, mesh=mesh, in_specs=in_specs, out_specs=out_specs, check_vma=False)
```

profile of v0, /device:TPU:1, one launch (start us, length us, event | category | flops | bytes accessed | tf_op | source)
XLA Modules:
  0.0 1727.1 jit_solution(12191001316250565196)
XLA Ops:
  7.2 1.2 convert_reduce_fusion
  8.6 204.1 %psum.63 = f32[32]{0:T(128)S(1)} all-reduce(f32[32]{0:T(128)S(1)} %reduce_sum.105), channel_id=1, replica_groups=mesh['batch'=8,'frame'=4,'row'=16] {'frame','row'}, use_global_device_ids=true, to_apply=%region_2.0 | all-reduce | flops 32 | bytes 256 | tf_op jit(solution)/shard_map/psum | solution.py:47
  212.9 1.1 fusion.103
  214.2 187.6 %psum.64 = f32[32]{0:T(128)S(1)} all-reduce(f32[32]{0:T(128)S(1)} %reduce_sum.111), channel_id=1, replica_groups=mesh['batch'=8,'frame'=4,'row'=16] {'frame','row'}, use_global_device_ids=true, to_apply=%region_5.6 | all-reduce | flops 32 | bytes 256 | tf_op jit(solution)/shard_map/psum | solution.py:49
  402.1 1.1 fusion.94
  403.2 3.5 collective-permute-start
  406.8 1.3 collective-permute-start.1
  408.1 3.6 collective-permute-done.1
  411.7 1.3 collective-permute-start.2
  413.1 2.2 collective-permute-done.2
  415.4 1.0 pad_slice_fusion.19
  421.7 189.3 %psum.65 = f32[32]{0:T(128)S(1)} all-reduce(f32[32]{0:T(128)S(1)} %reduce_sum.114), channel_id=1, replica_groups=mesh['batch'=8,'frame'=4,'row'=16] {'frame','row'}, use_global_device_ids=true, to_apply=%region_8.9 | all-reduce | flops 32 | bytes 256 | tf_op jit(solution)/shard_map/psum | solution.py:47
  611.6 187.5 %psum.66 = f32[32]{0:T(128)S(1)} all-reduce(f32[32]{0:T(128)S(1)} %reduce_sum.120), channel_id=1, replica_groups=mesh['batch'=8,'frame'=4,'row'=16] {'frame','row'}, use_global_device_ids=true, to_apply=%region_11.12 | all-reduce | flops 32 | bytes 256 | tf_op jit(solution)/shard_map/psum | solution.py:49
  799.9 3.0 collective-permute-start.3
  802.9 1.3 collective-permute-start.4
  804.4 2.8 collective-permute-done.4
  807.4 1.7 slice.841
  809.1 1.7 slice.839
  810.8 1.7 slice.843
  812.6 1.7 slice.845
  814.3 1.7 slice.847
  816.0 1.7 slice.849
  817.8 1.7 slice.851
  819.5 1.7 slice.853
  821.2 1.7 slice.855
  823.0 1.7 slice.857
  824.7 1.7 slice.859
  826.4 1.7 slice.861
  828.2 1.9 slice.863
  830.1 1.9 slice.865
  832.0 1.9 slice.867
  833.9 1.9 slice.869
  839.5 1.9 collective-permute-start.5
  841.4 1.3 collective-permute-start.6
  842.7 3.2 collective-permute-done.6
  846.0 1.3 slice.875
  847.2 1.2 slice.873
  848.5 1.2 slice.877
  849.7 1.2 slice.879
  855.1 1.3 slice.935
  856.4 0.8 fusion.209
  857.3 0.8 convolution_add_fusion.97
  858.1 0.8 convolution_add_fusion.96
  858.9 0.8 convolution_add_fusion.95
  863.3 1.9 collective-permute-start.7
  865.3 1.3 collective-permute-start.8
  866.6 3.3 collective-permute-done.8
  874.9 1.3 collective-permute-start.10
  876.2 6.3 collective-permute-start.9
  882.7 0.8 copy.56
  883.4 0.8 copy.57
  896.6 192.8 %all-reduce.7 = (f32[32]{0:T(128)S(1)}, f32[32]{0:T(128)S(1)}) all-reduce(f32[32]{0:T(128)S(1)} %reduce_sum.154, f32[32]{0:T(128)S(1)} %reduce_sum.126), channel_id=1, replica_groups=mesh['batch'=8,'frame'=4,'row'=16] {'frame','row'}, use_global_device_ids=true, to_apply=%region_17.18 | all-reduce | flops 64 | bytes 512 | tf_op jit(solution)/shard_map/psum | solution.py:57
  1096.0 1.3 collective-permute-start.11
  1097.3 1.4 collective-permute-start.12
  1099.7 2.4 collective-permute-done.12
  1102.1 1.5 collective-permute-start.13
  1104.1 1.2 copy-done.5
  1105.3 2.9 collective-permute-done.13
  1108.3 1.1 pad_slice_fusion.1
  1116.3 187.6 %all-reduce.6 = (f32[32]{0:T(128)S(1)}, f32[32]{0:T(128)S(1)}) all-reduce(f32[32]{0:T(128)S(1)} %reduce_sum.160, f32[32]{0:T(128)S(1)} %reduce_sum.157), channel_id=1, replica_groups=mesh['batch'=8,'frame'=4,'row'=16] {'frame','row'}, use_global_device_ids=true, to_apply=%region_23.24 | all-reduce | flops 64 | bytes 512 | tf_op jit(solution)/shard_map/psum | solution.py:57
  1304.3 1.0 fusion.106
  1305.3 410.3 %all-reduce.10.cloned.1.call-done = f32[442368]{0:T(1024)} async-done(((f32[442368]{0:T(1024)}), f32[442368]{0:T(1024)}) %all-reduce.10.cloned.1.call-update) | async-done | bytes 1769488 | tf_op jit(solution)/shard_map/psum | solution.py:253
  1715.6 2.7 multiply_reduce_fusion
  1718.9 1.3 broadcast_multiply_fusion
  (444 shorter events, 50.7 us)
Async XLA Ops:
  7.2 792.2 %copy-start = (bf16[128,3]{0,1:T(4,128)(2,1)S(1)}, bf16[128,3]{0,1:T(4,128)(2,1)}, u32[]{:S(2)}) copy-start(bf16[128,3]{0,1:T(4,128)(2,1)} %param.12) | copy-start | bytes 2308
  7.2 405.9 %copy-start.3 = (bf16[3,3,3,128,128]{4,3,2,1,0:T(8,128)(2,1)S(1)}, bf16[3,3,3,128,128]{4,3,2,1,0:T(8,128)(2,1)}, u32[]{:S(2)}) copy-start(bf16[3,3,3,128,128]{4,3,2,1,0:T(8,128)(2,1)} %param.10) | copy-start | bytes 2654212
  7.2 1708.4 %all-reduce.10.cloned.1.call-start = ((), (), s32[]{:S(2)}) async-start(), calls=%async_computation | async-start | bytes 3538944 | tf_op jit(solution)/shard_map/psum | solution.py:253
  212.9 193.8 %copy-start.74 = (f32[128]{0:T(128)}, f32[128]{0:T(128)S(1)}, u32[]{:S(2)}) copy-start(f32[128]{0:T(128)S(1)} %sub.64) | copy-start | bytes 1540
  402.1 4.7 copy-start.78
  403.2 4.8 collective-permute-start
  406.8 5.0 collective-permute-start.1
  411.7 3.5 collective-permute-start.2
  416.6 3.6 copy-start.6
  416.6 3.6 copy-start.8
  421.1 378.3 %copy-start.100 = (f32[128]{0:T(128)S(1)}, f32[128]{0:T(128)}, u32[]{:S(2)}) copy-start(f32[128]{0:T(128)} %param.11) | copy-start | bytes 1540
  611.2 188.6 %copy-start.72 = (f32[128]{0:T(128)}, f32[128]{0:T(128)S(1)}, u32[]{:S(2)}) copy-start(f32[128]{0:T(128)S(1)} %sub.69) | copy-start | bytes 1540
  611.2 193.0 %copy-start.58 = (bf16[1,4,4,3,64]{4,2,3,1,0:T(4,128)(2,1)S(1)}, bf16[1,4,4,3,64]{4,2,3,1,0:T(4,128)(2,1)}, u32[]{:S(2)}) copy-start(bf16[1,4,4,3,64]{4,2,3,1,0:T(4,128)(2,1)} %param.13) | copy-start | bytes 18436
  799.4 14.9 copy-start.76
  799.9 4.5 collective-permute-start.3
  802.9 4.4 collective-permute-start.4
  804.3 31.8 %copy-start.92 = (bf16[1,1,1,3,64]{4,2,3,1,0:T(2,128)(2,1)}, bf16[1,1,1,3,64]{4,2,3,1,0:T(2,128)(2,1)S(1)}, u32[]{:S(2)}) copy-start(bf16[1,1,1,3,64]{4,2,3,1,0:T(2,128)(2,1)S(1)} %get-tuple-element.100) | copy-start | bytes 1156
  804.3 32.2 %copy-start.96 = (bf16[1,1,1,3,64]{4,2,3,1,0:T(2,128)(2,1)}, bf16[1,1,1,3,64]{4,2,3,1,0:T(2,128)(2,1)S(1)}, u32[]{:S(2)}) copy-start(bf16[1,1,1,3,64]{4,2,3,1,0:T(2,128)(2,1)S(1)} %get-tuple-element.101) | copy-start | bytes 1156
  804.3 33.8 %copy-start.63 = (bf16[1,1,1,3,64]{4,2,3,1,0:T(2,128)(2,1)}, bf16[1,1,1,3,64]{4,2,3,1,0:T(2,128)(2,1)S(1)}, u32[]{:S(2)}) copy-start(bf16[1,1,1,3,64]{4,2,3,1,0:T(2,128)(2,1)S(1)} %get-tuple-element.94) | copy-start | bytes 1156
  804.3 33.8 %copy-start.65 = (bf16[1,1,1,3,64]{4,2,3,1,0:T(2,128)(2,1)}, bf16[1,1,1,3,64]{4,2,3,1,0:T(2,128)(2,1)S(1)}, u32[]{:S(2)}) copy-start(bf16[1,1,1,3,64]{4,2,3,1,0:T(2,128)(2,1)S(1)} %get-tuple-element.95) | copy-start | bytes 1156
  804.3 33.8 %copy-start.67 = (bf16[1,1,1,3,64]{4,2,3,1,0:T(2,128)(2,1)}, bf16[1,1,1,3,64]{4,2,3,1,0:T(2,128)(2,1)S(1)}, u32[]{:S(2)}) copy-start(bf16[1,1,1,3,64]{4,2,3,1,0:T(2,128)(2,1)S(1)} %get-tuple-element.98) | copy-start | bytes 1156
  804.3 33.8 %copy-start.69 = (bf16[1,1,1,3,64]{4,2,3,1,0:T(2,128)(2,1)}, bf16[1,1,1,3,64]{4,2,3,1,0:T(2,128)(2,1)S(1)}, u32[]{:S(2)}) copy-start(bf16[1,1,1,3,64]{4,2,3,1,0:T(2,128)(2,1)S(1)} %get-tuple-element.99) | copy-start | bytes 1156
  804.3 33.8 %copy-start.84 = (bf16[1,1,1,3,64]{4,2,3,1,0:T(2,128)(2,1)}, bf16[1,1,1,3,64]{4,2,3,1,0:T(2,128)(2,1)S(1)}, u32[]{:S(2)}) copy-start(bf16[1,1,1,3,64]{4,2,3,1,0:T(2,128)(2,1)S(1)} %get-tuple-element.96) | copy-start | bytes 1156
  804.3 33.8 %copy-start.88 = (bf16[1,1,1,3,64]{4,2,3,1,0:T(2,128)(2,1)}, bf16[1,1,1,3,64]{4,2,3,1,0:T(2,128)(2,1)S(1)}, u32[]{:S(2)}) copy-start(bf16[1,1,1,3,64]{4,2,3,1,0:T(2,128)(2,1)S(1)} %get-tuple-element.97) | copy-start | bytes 1156
  804.3 33.8 %copy-start.90 = (bf16[1,1,1,3,64]{4,2,3,1,0:T(2,128)(2,1)}, bf16[1,1,1,3,64]{4,2,3,1,0:T(2,128)(2,1)S(1)}, u32[]{:S(2)}) copy-start(bf16[1,1,1,3,64]{4,2,3,1,0:T(2,128)(2,1)S(1)} %get-tuple-element.92) | copy-start | bytes 1156
  804.3 33.8 %copy-start.94 = (bf16[1,1,1,3,64]{4,2,3,1,0:T(2,128)(2,1)}, bf16[1,1,1,3,64]{4,2,3,1,0:T(2,128)(2,1)S(1)}, u32[]{:S(2)}) copy-start(bf16[1,1,1,3,64]{4,2,3,1,0:T(2,128)(2,1)S(1)} %get-tuple-element.93) | copy-start | bytes 1156
  804.4 33.8 %copy-start.61 = (bf16[1,1,1,3,64]{4,2,3,1,0:T(2,128)(2,1)}, bf16[1,1,1,3,64]{4,2,3,1,0:T(2,128)(2,1)S(1)}, u32[]{:S(2)}) copy-start(bf16[1,1,1,3,64]{4,2,3,1,0:T(2,128)(2,1)S(1)} %get-tuple-element.91) | copy-start | bytes 1156
  804.4 34.0 %copy-start.59 = (bf16[1,1,1,3,64]{4,2,3,1,0:T(2,128)(2,1)}, bf16[1,1,1,3,64]{4,2,3,1,0:T(2,128)(2,1)S(1)}, u32[]{:S(2)}) copy-start(bf16[1,1,1,3,64]{4,2,3,1,0:T(2,128)(2,1)S(1)} %get-tuple-element.90) | copy-start | bytes 1156
  804.4 34.2 %copy-start.86 = (bf16[1,1,1,3,64]{4,2,3,1,0:T(2,128)(2,1)}, bf16[1,1,1,3,64]{4,2,3,1,0:T(2,128)(2,1)S(1)}, u32[]{:S(2)}) copy-start(bf16[1,1,1,3,64]{4,2,3,1,0:T(2,128)(2,1)S(1)} %get-tuple-element.89) | copy-start | bytes 1156
  804.4 34.4 %copy-start.82 = (bf16[1,1,1,3,64]{4,2,3,1,0:T(2,128)(2,1)}, bf16[1,1,1,3,64]{4,2,3,1,0:T(2,128)(2,1)S(1)}, u32[]{:S(2)}) copy-start(bf16[1,1,1,3,64]{4,2,3,1,0:T(2,128)(2,1)S(1)} %get-tuple-element.88) | copy-start | bytes 1156
  804.4 34.8 %copy-start.80 = (bf16[1,1,1,3,64]{4,2,3,1,0:T(2,128)(2,1)}, bf16[1,1,1,3,64]{4,2,3,1,0:T(2,128)(2,1)S(1)}, u32[]{:S(2)}) copy-start(bf16[1,1,1,3,64]{4,2,3,1,0:T(2,128)(2,1)S(1)} %get-tuple-element.86) | copy-start | bytes 1156
  837.8 18.6 %copy-start.4 = (bf16[2,4,4,64,128]{4,3,2,1,0:T(8,128)(2,1)S(1)}, bf16[2,4,4,64,128]{4,3,2,1,0:T(8,128)(2,1)}, u32[]{:S(2)}) copy-start(bf16[2,4,4,64,128]{4,3,2,1,0:T(8,128)(2,1)} %param.14) | copy-start | bytes 1572868
  839.5 3.2 collective-permute-start.5
  841.4 4.5 collective-permute-start.6
  856.4 6.7 copy-start.71
  856.4 6.7 copy-start.99
  863.3 3.2 collective-permute-start.7
  865.3 4.6 collective-permute-start.8
  874.9 13.9 collective-permute-start.10
  876.2 12.7 collective-permute-start.9
  882.6 6.3 copy-start.70
  882.6 6.6 copy-start.68
  882.6 7.0 copy-start.66
  882.6 7.3 copy-start.64
  882.6 7.6 copy-start.97
  882.6 7.9 copy-start.95
  882.6 8.2 copy-start.62
  883.4 7.8 copy-start.93
  884.2 7.4 copy-start.91
  884.9 7.0 copy-start.60
  885.7 6.5 copy-start.89
  886.4 6.2 copy-start.87
  887.9 5.3 copy-start.85
  888.7 4.9 copy-start.83
  888.8 5.1 copy-start.81
  892.2 3.5 copy-start.73
  892.2 3.5 copy-start.77
  892.3 3.5 copy-start.101
  895.7 194.3 %copy-start.39 = (bf16[4,8,32,128]{3,2,1,0:T(8,128)(2,1)S(1)}, bf16[4,8,32,128]{3,2,1,0:T(8,128)(2,1)}, u32[]{:S(2)}) copy-start(bf16[4,8,32,128]{3,2,1,0:T(8,128)(2,1)} %copy-done.38) | copy-start | bytes 786436
  895.7 194.3 %copy-start.47 = (bf16[4,8,32,128]{3,2,1,0:T(8,128)(2,1)S(1)}, bf16[4,8,32,128]{3,2,1,0:T(8,128)(2,1)}, u32[]{:S(2)}) copy-start(bf16[4,8,32,128]{3,2,1,0:T(8,128)(2,1)} %copy-done.46) | copy-start | bytes 786436
  895.7 194.3 %copy-start.49 = (bf16[4,8,32,128]{3,2,1,0:T(8,128)(2,1)S(1)}, bf16[4,8,32,128]{3,2,1,0:T(8,128)(2,1)}, u32[]{:S(2)}) copy-start(bf16[4,8,32,128]{3,2,1,0:T(8,128)(2,1)} %copy-done.48) | copy-start | bytes 786436
  1096.0 3.7 collective-permute-start.11
  1097.3 4.8 collective-permute-start.12
  1102.1 6.1 collective-permute-start.13
  (53 other events, 79.6 us)
Sparse Core Ops, SparseCore 0:
  1105.4 610.0 all-reduce.9
where the time goes:
time: 1730 us
  blocking collectives  1150 us (66%)
  waiting for transfers between devices  431 us (25%)
  local copies, waits for them, and re-layouts  59.7 us (3%)
  matrix products  31.4 us (2%)
  starting transfers between devices  28.7 us (2%)
    psum x1, waiting for transfers between devices, shards(): summed_weight = lax.psum(local_weight, ('batch', 'frame', 'row'))  410 us
    psum x2, blocking collectives, norm_forward(): totals = lax.psum(group_sums(values, groups), ('frame', 'row'))  393 us
    psum x2, blocking collectives, norm_backward(): lax.psum((group_sums(weighted, groups), group_sums(weighted * normed, gro...  380 us
    psum x2, blocking collectives, norm_forward(): lax.psum(group_sums(centred * centred, groups), ('frame', 'row'))  375 us
    slice x48, local copies, waits for them, and re-layouts, strided_conv(): extended[tap_t::time_taps, tap_r:tap_r + 2 * rows_out:2, tap_c:tap_c + 2...  38.6 us
  transfers between devices with their start and end apart: 15, of which 8 were waited for; matrix products, arithmetic and copies ran while one was open for 1% of the time, Pallas kernels for 0%

commit v1 on v0

--- a/solution.py
+++ b/solution.py
@@ -1,12 +1,256 @@
+import functools
+
 import jax
 import jax.numpy as jnp
 from jax import lax
+from jax.experimental import pallas as pl
+from jax.experimental.pallas import tpu as pltpu
 from jax.sharding import PartitionSpec as P
 
 GROUPS = 32
 
 
 EPSILON = 1e-06
+
+def group_total(values):
+    lane = lax.broadcasted_iota(jnp.int32, values.shape, 1)
+    paired = values + jnp.where(
+        lane % 2 == 0, pltpu.roll(values, 127, 1), pltpu.roll(values, 1, 1)
+    )
+    return paired + jnp.where(
+        lane % 4 < 2, pltpu.roll(paired, 126, 1), pltpu.roll(paired, 2, 1)
+    )
+
+
+def place():
+    batch = lax.axis_index("batch")
+    row = lax.axis_index("row")
+    return dict(
+        batch=batch,
+        z_lo=batch // 2,
+        core=batch % 2,
+        frame=lax.axis_index("frame"),
+        row=row,
+        z_hi=row // 4,
+        y=row % 4,
+    )
+
+
+def device(me, **changed):
+    at = dict(me, **changed)
+    return (at["z_lo"] * 2 + at["core"], at["frame"], at["z_hi"] * 4 + at["y"])
+
+
+def plane_peers(me):
+    own = me["frame"] * 4 + me["y"]
+    for step in range(1, 16):
+        other = (own + step) % 16
+        yield device(me, frame=other // 4, y=other % 4)
+
+
+def high_peers(me):
+    for step in range(1, 4):
+        yield device(me, z_hi=(me["z_hi"] + step) % 4)
+
+
+def broadcast_slot(buffer, slot, peers, send_sem, recv_sem):
+    copies = []
+    for peer in peers:
+        copy = pltpu.make_async_remote_copy(
+            src_ref=buffer.at[slot],
+            dst_ref=buffer.at[slot],
+            send_sem=send_sem,
+            recv_sem=recv_sem,
+            device_id=peer,
+            device_id_type=pl.DeviceIdType.MESH,
+        )
+        copy.start()
+        copies.append(copy)
+    return copies
+
+
+def wait_all(buffer, count, send_sem, recv_sem):
+    whole = buffer.at[pl.ds(0, count)]
+    pltpu.make_async_copy(whole, whole, recv_sem).wait()
+    pltpu.make_async_copy(whole, whole, send_sem).wait()
+
+
+def tile(row):
+    return jnp.broadcast_to(row, (8, row.shape[-1]))
+
+
+def enter(peers):
+    barrier = pltpu.get_barrier_semaphore()
+    for peer in peers:
+        pl.semaphore_signal(
+            barrier, inc=1, device_id=peer, device_id_type=pl.DeviceIdType.MESH
+        )
+    pl.semaphore_wait(barrier, len(peers))
+
+
+def merged_moments(slots, entries):
+    count = slots.shape[0]
+    means, squares = (slots[:, 0, :], slots[:, 1, :])
+    mean = group_total(tile(jnp.sum(means, axis=0, keepdims=True))) / (4 * count)
+    apart = means - mean[0:1]
+    total = jnp.sum(squares + entries * (apart * apart), axis=0, keepdims=True)
+    return (mean, group_total(tile(total)))
+
+
+def moments_kernel(entries, v_ref, o_ref, plane, high, send, recv):
+    me = place()
+    near, far = (list(plane_peers(me)), list(high_peers(me)))
+    enter(near + far)
+    slot = me["frame"] * 4 + me["y"]
+    plane[slot] = v_ref[...]
+    broadcast_slot(plane, slot, near, send.at[0], recv.at[0])
+    wait_all(plane, 15, send.at[0], recv.at[0])
+    mean, squares = merged_moments(plane[...], float(entries))
+    high[me["z_hi"], 0:1, :] = mean[0:1]
+    high[me["z_hi"], 1:2, :] = squares[0:1]
+    broadcast_slot(high, me["z_hi"], far, send.at[1], recv.at[1])
+    wait_all(high, 3, send.at[1], recv.at[1])
+    means, squares = (high[:, 0, :], high[:, 1, :])
+    mean = jnp.sum(means, axis=0, keepdims=True) / 4.0
+    apart = means - mean
+    total = jnp.sum(squares + (64.0 * entries) * (apart * apart), axis=0, keepdims=True)
+    o_ref[0:1, :] = mean
+    o_ref[1:2, :] = total / (256.0 * entries)
+
+
+def sums_kernel(v_ref, o_ref, plane, high, send, recv):
+    me = place()
+    near, far = (list(plane_peers(me)), list(high_peers(me)))
+    enter(near + far)
+    slot = me["frame"] * 4 + me["y"]
+    plane[slot] = v_ref[...]
+    broadcast_slot(plane, slot, near, send.at[0], recv.at[0])
+    wait_all(plane, 15, send.at[0], recv.at[0])
+    sums = jnp.sum(plane[...], axis=0)
+    high[me["z_hi"], 0:1, :] = group_total(tile(sums[0:1]))[0:1]
+    high[me["z_hi"], 1:2, :] = group_total(tile(sums[1:2]))[0:1]
+    broadcast_slot(high, me["z_hi"], far, send.at[1], recv.at[1])
+    wait_all(high, 3, send.at[1], recv.at[1])
+    o_ref[...] = jnp.sum(high[...], axis=0)
+
+
+def clip_exchange(kernel, values, collective_id):
+    lanes = values.shape[-1]
+    return pl.pallas_call(
+        kernel,
+        out_shape=jax.ShapeDtypeStruct(values.shape, jnp.float32),
+        in_specs=[pl.BlockSpec(memory_space=pltpu.VMEM)],
+        out_specs=pl.BlockSpec(memory_space=pltpu.VMEM),
+        scratch_shapes=[
+            pltpu.VMEM((16, 2, lanes), jnp.float32),
+            pltpu.VMEM((4, 2, lanes), jnp.float32),
+            pltpu.SemaphoreType.DMA((2,)),
+            pltpu.SemaphoreType.DMA((2,)),
+        ],
+        compiler_params=pltpu.CompilerParams(collective_id=collective_id, has_side_effects=True),
+    )(values)
+
+
+def z_peers(me):
+    own = me["z_hi"] * 4 + me["z_lo"]
+    for step in range(1, 16):
+        other = (own + step) % 16
+        yield device(me, z_hi=other // 4, z_lo=other % 4)
+
+
+def update_kernel(
+    w_ref, o_ref, pair_out, pair_in, x_out, x_in, y_out, y_in, z_out, z_in, z_all, gathered, send, recv
+):
+    me = place()
+    core, frame, y, z = (me["core"], me["frame"], me["y"], me["z_hi"] * 4 + me["z_lo"])
+    partner = [device(me, core=1 - core)]
+    line = list(z_peers(me))
+    x_others = [(frame + step) % 4 for step in range(1, 4)]
+    y_others = [(y + step) % 4 for step in range(1, 4)]
+    x_line = [device(me, frame=other) for other in x_others]
+    y_line = [device(me, y=other) for other in y_others]
+    enter(partner + x_line + y_line + line)
+
+    def push(src, dst, peer, stage):
+        pltpu.make_async_remote_copy(
+            src_ref=src,
+            dst_ref=dst,
+            send_sem=send.at[stage],
+            recv_sem=recv.at[stage],
+            device_id=peer,
+            device_id_type=pl.DeviceIdType.MESH,
+        ).start()
+
+    pair_out[...] = w_ref[1 - core].astype(jnp.bfloat16)
+    push(pair_out, pair_in, partner[0], 0)
+    wait_all(pair_out, 4, send.at[0], recv.at[0])
+    x_out[...] = (w_ref[core] + pair_in[...].astype(jnp.float32)).astype(jnp.bfloat16)
+    for other, peer in zip(x_others, x_line):
+        push(x_out.at[other], x_in.at[frame], peer, 1)
+    own = w_ref[core, frame] + pair_in[frame].astype(jnp.float32)
+    x_in[frame] = jnp.zeros(x_in.shape[1:], x_in.dtype)
+    wait_all(x_out, 3, send.at[1], recv.at[1])
+    own = own + jnp.sum(x_in[...].astype(jnp.float32), axis=0)
+    y_out[0:432, :] = own.astype(jnp.bfloat16)
+    y_out[432:448, :] = jnp.zeros((16, 128), jnp.bfloat16)
+    for other, peer in zip(y_others, y_line):
+        push(y_out.at[pl.ds(other * 112, 112)], y_in.at[y], peer, 2)
+    y_in[y] = y_out[pl.ds(y * 112, 112), :]
+    wait_all(y_in, 3, send.at[2], recv.at[2])
+    z_out[0:14] = jnp.sum(y_in[...].astype(jnp.float32), axis=0).reshape(14, 8, 128)
+    z_out[14:16] = jnp.zeros((2, 8, 128), jnp.float32)
+    for step, peer in enumerate(line):
+        push(z_out.at[(z + 1 + step) % 16], z_in.at[z], peer, 3)
+    z_in[z] = z_out[z]
+    wait_all(z_in, 15, send.at[3], recv.at[3])
+    z_all[z] = jnp.sum(z_in[...], axis=0)
+    broadcast_slot(z_all, z, line, send.at[4], recv.at[4])
+    wait_all(z_all, 15, send.at[4], recv.at[4])
+    mine = gathered.at[core, frame]
+    mine[y] = z_all[0:14].reshape(112, 128).astype(jnp.bfloat16)
+    broadcast_slot(mine, y, y_line, send.at[5], recv.at[5])
+    wait_all(mine, 3, send.at[5], recv.at[5])
+    half = gathered.at[core]
+    broadcast_slot(half, frame, x_line, send.at[6], recv.at[6])
+    wait_all(half, 3, send.at[6], recv.at[6])
+    broadcast_slot(gathered, core, partner, send.at[7], recv.at[7])
+    wait_all(gathered, 1, send.at[7], recv.at[7])
+    squares = jnp.zeros((8, 128), jnp.float32)
+    for part in range(8):
+        piece = gathered[part // 4, part % 4].reshape(448, 128)[0:432].astype(jnp.float32)
+        squares = squares + jnp.sum((piece * piece).reshape(54, 8, 128), axis=0)
+    mean = jnp.sum(squares, keepdims=True) / (8 * 432 * 128)
+    scale = lax.rsqrt(mean + EPSILON)
+    for part in range(8):
+        piece = gathered[part // 4, part % 4].reshape(448, 128)[0:432].astype(jnp.float32)
+        o_ref[part // 4, part % 4] = piece * scale
+
+
+def summed_update(local_weight):
+    low = jnp.bfloat16
+    return pl.pallas_call(
+        update_kernel,
+        out_shape=jax.ShapeDtypeStruct((2, 4, 432, 128), jnp.float32),
+        in_specs=[pl.BlockSpec(memory_space=pltpu.VMEM)],
+        out_specs=pl.BlockSpec(memory_space=pltpu.VMEM),
+        scratch_shapes=[
+            pltpu.VMEM((4, 432, 128), low),
+            pltpu.VMEM((4, 432, 128), low),
+            pltpu.VMEM((4, 432, 128), low),
+            pltpu.VMEM((4, 432, 128), low),
+            pltpu.VMEM((448, 128), low),
+            pltpu.VMEM((4, 112, 128), low),
+            pltpu.VMEM((16, 8, 128), jnp.float32),
+            pltpu.VMEM((16, 8, 128), jnp.float32),
+            pltpu.VMEM((16, 8, 128), jnp.float32),
+            pltpu.VMEM((2, 4, 4, 112, 128), low),
+            pltpu.SemaphoreType.DMA((8,)),
+            pltpu.SemaphoreType.DMA((8,)),
+        ],
+        compiler_params=pltpu.CompilerParams(
+            collective_id=3, has_side_effects=True, vmem_limit_bytes=40 * 1024 * 1024
+        ),
+    )(local_weight.reshape(2, 4, 432, 128))
 
 
 def with_halo(block, sides, width):
@@ -33,32 +277,24 @@
     return logistic * (1.0 + values * (1.0 - logistic))
 
 
-def group_sums(values, groups):
-    shaped = values.reshape(values.shape[:-1] + (groups, values.shape[-1] // groups))
-    return jnp.sum(shaped, axis=(0, 1, 2, 4))
-
-
-def spread_channels(per_group, channel_count):
-    return jnp.repeat(per_group, channel_count // per_group.shape[0])
-
-
 def norm_forward(values, groups, member_count):
-    channel_count = values.shape[-1]
-    totals = lax.psum(group_sums(values, groups), ("frame", "row"))
-    centred = values - spread_channels(totals / member_count, channel_count)
-    variance = lax.psum(group_sums(centred * centred, groups), ("frame", "row")) / member_count
-    inverse = spread_channels(lax.rsqrt(variance + EPSILON), channel_count)
-    return (centred * inverse, inverse)
+    channels = values.shape[-1]
+    entries = values.size // channels
+    mean = jnp.mean(values, axis=(0, 1, 2))
+    centred = values - mean
+    squares = jnp.sum(centred * centred, axis=(0, 1, 2))
+    kernel = functools.partial(moments_kernel, entries)
+    mean, variance = clip_exchange(kernel, jnp.stack([mean, squares]), 1)
+    inverse = lax.rsqrt(variance + EPSILON)
+    return ((values - mean) * inverse, inverse)
 
 
 def norm_backward(act_grad, scaled, normed, inverse, gain, groups, member_count):
-    channel_count = normed.shape[-1]
     weighted = act_grad * silu_slope(scaled) * gain
-    first_sum, second_sum = lax.psum(
-        (group_sums(weighted, groups), group_sums(weighted * normed, groups)), ("frame", "row")
-    )
-    first_mean = spread_channels(first_sum / member_count, channel_count)
-    second_mean = spread_channels(second_sum / member_count, channel_count)
+    local = jnp.stack(
+        [jnp.sum(weighted, axis=(0, 1, 2)), jnp.sum(weighted * normed, axis=(0, 1, 2))]
+    )
+    first_mean, second_mean = clip_exchange(sums_kernel, local, 2) / member_count
     return (weighted - first_mean - normed * second_mean) * inverse
 
 
@@ -250,8 +486,7 @@
             member_count,
         )
     ).astype(jnp.bfloat16)
-    summed_weight = lax.psum(local_weight, ("batch", "frame", "row"))
-    update = summed_weight * lax.rsqrt(jnp.mean(summed_weight * summed_weight) + EPSILON)
+    update = summed_update(local_weight)
     return (input_grad[None], update.reshape(conv_weight.shape))
 
 

time: 1730 us -> 328 us (0.19)
  blocking collectives: 1150 us -> 0 us
  waiting for transfers between devices: 431 us -> 21.4 us
  Pallas kernels: 0 us -> 171 us
    psum x6 -> x0, blocking collectives: 1150 us -> none  [the longest x2 393 us: norm_forward(): totals = lax.psum(group_sums(values, groups), ('frame', 'row'))]
    psum x1 -> x0, waiting for transfers between devices: 410 us -> none  [shards(): summed_weight = lax.psum(local_weight, ('batch', 'frame', 'row'))]
    pallas_call x0 -> x5, Pallas kernels: none -> 171 us  [the longest x4 102 us: clip_exchange(): pl.pallas_call(kernel, out_shape=jax.ShapeDtypeStruct(values.shape, jnp.f...]
  transfers between devices with their start and end apart: 15 -> 14, of which waited for: 8 -> 6; matrix products, arithmetic and copies ran while one was open for 1% -> 2% of each run, Pallas kernels for 0% -> 21%
where the time goes in v1:
time: 328 us; the launch traced here: 327 us
  Pallas kernels  171 us (52%)
  local copies, waits for them, and re-layouts  51 us (16%)
  starting transfers between devices  39.2 us (12%)
  matrix products  30.4 us (9%)
  waiting for transfers between devices  21.4 us (7%)
  other arithmetic  11.7 us (4%)
    pallas_call x4, Pallas kernels, clip_exchange(): pl.pallas_call(kernel, out_shape=jax.ShapeDtypeStruct(values.shape, jnp.f...  102 us
    pallas_call x1, Pallas kernels, summed_update(): pl.pallas_call(update_kernel, out_shape=jax.ShapeDtypeStruct((2, 4, 432,...  68.8 us
    slice x48, local copies, waits for them, and re-layouts, strided_conv(): extended[tap_t::time_taps, tap_r:tap_r + 2 * rows_out:2, tap_c:tap_c + 2...  33.1 us
    ppermute x6, starting transfers between devices, with_halo(): lax.ppermute(lax.slice_in_dim(block, block.shape[dim] - width, None, axis...  27.6 us
    ppermute x6, waiting for transfers between devices, with_halo(): lax.ppermute(lax.slice_in_dim(block, 0, width, axis=dim), axis, backward)  19.2 us
    dot_general x48, matrix products, strided_back(): jnp.dot(source, weight[tap_t, tap_r, tap_c].T, preferred_element_type=jnp...  9.65 us
    unnamed x162, local copies, waits for them, and re-layouts  8.06 us
    ppermute x6, starting transfers between devices, with_halo(): lax.ppermute(lax.slice_in_dim(block, 0, width, axis=dim), axis, backward)  7.88 us
  transfers between devices with their start and end apart: 14, of which 6 were waited for; matrix products, arithmetic and copies ran while one was open for 2% of the time, Pallas kernels for 21%

profile of v1, /device:TPU:1, one launch (start us, length us, event | category | flops | bytes accessed | tf_op | source)
XLA Modules:
  0.0 327.1 jit_solution(15016050504520582047)
XLA Ops:
  0.7 1.2 convert_reduce_fusion
  1.8 1.1 fusion.86
  3.5 26.4 %shard_map.95 = f32[2,128]{1,0:T(2,128)} custom-call(f32[2,128]{1,0:T(2,128)} %pad_maximum_fusion.34.v_ref), custom_call_target="tpu_custom_call" | custom-call | tf_op jit(solution)/shard_map/pallas_call | solution.py:139
  29.9 0.7 slice_bitcast_fusion.5
  30.7 1.1 fusion.97
  31.8 2.3 collective-permute-start
  34.2 1.3 collective-permute-start.1
  35.5 3.3 %collective-permute-done.1 = bf16[4,1,32,128]{3,2,1,0:T(8,128)(2,1)S(1)} collective-permute-done((bf16[4,1,32,128]{3,2,1,0:T(8,128)(2,1)S(1)}, bf16[4,1,32,128]{3,2,1,0:T(8,128)(2,1)S(1)}, u32[]{:S(2)}, u32[]{:S(2)}) %collective-permute-start.1) | collective-permute-done | bytes 32800 | tf_op jit(solution)/shard_map/ppermute | solution.py:264
  38.8 2.2 collective-permute-start.2
  41.1 2.2 collective-permute-done.2
  43.3 0.9 pad_slice_fusion.19
  50.0 28.2 %shard_map.96 = f32[2,128]{1,0:T(2,128)} custom-call(f32[2,128]{1,0:T(2,128)} %pad_maximum_fusion.35.v_ref), custom_call_target="tpu_custom_call" | custom-call | tf_op jit(solution)/shard_map/pallas_call | solution.py:139
  78.2 0.7 slice_bitcast_fusion.4
  79.4 2.5 collective-permute-start.3
  81.9 1.3 collective-permute-start.4
  83.4 2.9 collective-permute-done.4
  86.4 1.7 slice.841
  88.1 1.7 slice.839
  89.8 1.7 slice.843
  91.6 1.7 slice.845
  93.3 1.7 slice.847
  95.0 1.7 slice.849
  96.8 1.7 slice.851
  98.5 1.7 slice.853
  100.2 1.7 slice.855
  102.0 1.7 slice.857
  103.7 1.7 slice.859
  105.4 1.7 slice.861
  107.2 1.9 slice.863
  109.1 1.9 slice.865
  111.0 1.9 slice.867
  112.9 1.9 slice.869
  118.5 2.2 collective-permute-start.5
  120.7 1.3 collective-permute-start.6
  122.0 7.4 %collective-permute-done.6 = bf16[4,1,16,64]{3,2,1,0:T(8,128)(2,1)S(1)} collective-permute-done((bf16[4,1,16,64]{3,2,1,0:T(8,128)(2,1)S(1)}, bf16[4,1,16,64]{3,2,1,0:T(8,128)(2,1)S(1)}, u32[]{:S(2)}, u32[]{:S(2)}) %collective-permute-start.6) | collective-permute-done | bytes 8224 | tf_op jit(solution)/shard_map/ppermute | solution.py:264
  138.7 9.4 %collective-permute-start.7 = (bf16[2,1,8,128]{3,2,1,0:T(8,128)(2,1)S(1)}, bf16[2,1,8,128]{3,2,1,0:T(8,128)(2,1)S(1)}, u32[]{:S(2)}, u32[]{:S(2)}) collective-permute-start(bf16[2,1,8,128]{3,2,1,0:T(8,128)(2,1)S(1)} %get-tuple-element.98), channel_id=1, source_target_pairs={{0,1},{1,2},{2,3},{3,4},{4,5},{5,6},{6,7},{7,8},{8,9},{9,10},{10,1... | collective-permute-start | bytes 12296 | tf_op jit(solution)/shard_map/ppermute | solution.py:261
  148.0 1.3 collective-permute-start.8
  149.4 3.0 collective-permute-done.8
  157.3 1.3 collective-permute-start.10
  158.7 8.7 %collective-permute-start.9 = (bf16[4,1,16,64]{3,2,1,0:T(8,128)(2,1)S(1)}, bf16[4,1,16,64]{3,2,1,0:T(8,128)(2,1)S(1)}, u32[]{:S(2)}, u32[]{:S(2)}) collective-permute-start(bf16[4,1,16,64]{3,2,1,0:T(8,128)(2,1)S(1)} %get-tuple-element.76), channel_id=1, source_target_pairs={{0,1},{1,2},{2,3},{3,4},{4,5},{5,6},{6,7},{7,8},{8,9},{9,10},{10,1... | collective-permute-start | bytes 24584 | tf_op jit(solution)/shard_map/ppermute | solution.py:261
  167.5 0.7 copy.56
  168.3 0.7 copy.57
  169.0 0.7 copy.58
  169.8 0.7 copy.59
  170.5 0.7 copy.60
  171.2 0.7 copy.61
  172.0 0.7 copy.62
  172.7 0.7 copy.63
  180.9 0.6 pad_maximum_fusion.36.v_ref
  181.5 29.5 %shard_map.97 = f32[2,128]{1,0:T(2,128)} custom-call(f32[2,128]{1,0:T(2,128)} %pad_maximum_fusion.36.v_ref), custom_call_target="tpu_custom_call" | custom-call | tf_op jit(solution)/shard_map/pallas_call | solution.py:139
  211.0 0.7 broadcast_multiply_fusion.1
  211.8 1.4 fusion.14
  218.1 2.5 collective-permute-start.11
  220.7 1.4 collective-permute-start.12
  223.0 2.4 collective-permute-done.12
  225.5 1.5 collective-permute-start.13
  227.5 68.8 %shard_map.99 = f32[2,4,432,128]{3,2,1,0:T(8,128)S(1)} custom-call(f32[2,4,432,128]{3,2,1,0:T(8,128)S(1)} %bitcast.800), custom_call_target="tpu_custom_call" | custom-call | tf_op jit(solution)/shard_map/pallas_call | solution.py:231
  296.4 1.1 pad_slice_fusion.1
  297.7 0.7 copy-done.56
  303.5 1.3 fusion.351
  305.3 17.9 %shard_map.98 = f32[2,128]{1,0:T(2,128)} custom-call(f32[2,128]{1,0:T(2,128)} %pad_maximum_fusion.37.v_ref), custom_call_target="tpu_custom_call" | custom-call | tf_op jit(solution)/shard_map/pallas_call | solution.py:139
  323.2 0.7 broadcast_multiply_fusion
  323.9 2.0 fusion.107
  325.9 1.2 copy.217
  (367 shorter events, 43.5 us)
Async XLA Ops:
  0.6 78.3 %copy-start = (bf16[128,3]{0,1:T(4,128)(2,1)S(1)}, bf16[128,3]{0,1:T(4,128)(2,1)}, u32[]{:S(2)}) copy-start(bf16[128,3]{0,1:T(4,128)(2,1)} %param.12) | copy-start | bytes 2308
  0.6 40.4 %copy-start.2 = (bf16[3,3,3,128,128]{4,3,2,1,0:T(8,128)(2,1)S(1)}, bf16[3,3,3,128,128]{4,3,2,1,0:T(8,128)(2,1)}, u32[]{:S(2)}) copy-start(bf16[3,3,3,128,128]{4,3,2,1,0:T(8,128)(2,1)} %param.10) | copy-start | bytes 2654212
  31.8 3.6 %collective-permute-start = (bf16[4,1,32,128]{3,2,1,0:T(8,128)(2,1)S(1)}, bf16[4,1,32,128]{3,2,1,0:T(8,128)(2,1)S(1)}, u32[]{:S(2)}, u32[]{:S(2)}) collective-permute-start(bf16[4,1,32,128]{3,2,1,0:T(8,128)(2,1)S(1)} %get-tuple-element.74), channel_id=1, source_target_pairs={{0,1},{1,2},{2,3},{3,4},{4,5},{5,6},{6,7},{7,8},{8,9},{9,10},{10,1... | collective-permute-start | bytes 98312 | tf_op jit(solution)/shard_map/ppermute | solution.py:261
  34.2 4.7 %collective-permute-start.1 = (bf16[4,1,32,128]{3,2,1,0:T(8,128)(2,1)S(1)}, bf16[4,1,32,128]{3,2,1,0:T(8,128)(2,1)S(1)}, u32[]{:S(2)}, u32[]{:S(2)}) collective-permute-start(bf16[4,1,32,128]{3,2,1,0:T(8,128)(2,1)S(1)} %get-tuple-element.75), channel_id=1, source_target_pairs={{1,0},{2,1},{3,2},{4,3},{5,4},{6,5},{7,6},{8,7},{9,8},{10,9},{11,1... | collective-permute-start | bytes 98312 | tf_op jit(solution)/shard_map/ppermute | solution.py:264
  38.8 4.4 %collective-permute-start.2 = (bf16[2,10,32,128]{3,2,1,0:T(8,128)(2,1)S(1)}, bf16[2,10,32,128]{3,2,1,0:T(8,128)(2,1)S(1)}, u32[]{:S(2)}, u32[]{:S(2)}) collective-permute-start(bf16[2,10,32,128]{3,2,1,0:T(8,128)(2,1)S(1)} %pad_maximum_fusion.31), channel_id=1, source_target_pairs={{0,16},{16,32},{32,48},{1,17},{17,33},{33,49},{2,18},{18,34},{34,5... | collective-permute-start | bytes 491528 | tf_op jit(solution)/shard_map/ppermute | solution.py:272
  44.2 1.5 copy-start.30
  44.3 1.5 copy-start.32
  44.3 2.0 copy-start.26
  44.3 2.0 copy-start.28
  44.3 2.4 copy-start.20
  44.3 2.4 copy-start.22
  44.3 2.4 copy-start.24
  44.3 2.7 copy-start.14
  44.3 2.7 copy-start.16
  44.3 2.7 copy-start.18
  44.3 3.1 copy-start.10
  44.4 3.1 copy-start.12
  44.4 3.5 %copy-start.6 = (bf16[4,8,32,128]{3,2,1,0:T(8,128)(2,1)}, bf16[4,8,32,128]{3,2,1,0:T(8,128)(2,1)S(1)}, u32[]{:S(2)}) copy-start(bf16[4,8,32,128]{3,2,1,0:T(8,128)(2,1)S(1)} %get-tuple-element.62) | copy-start | bytes 786436
  44.4 3.5 %copy-start.8 = (bf16[4,8,32,128]{3,2,1,0:T(8,128)(2,1)}, bf16[4,8,32,128]{3,2,1,0:T(8,128)(2,1)S(1)}, u32[]{:S(2)}) copy-start(bf16[4,8,32,128]{3,2,1,0:T(8,128)(2,1)S(1)} %get-tuple-element.63) | copy-start | bytes 786436
  44.4 3.9 %copy-start.4 = (bf16[4,8,32,128]{3,2,1,0:T(8,128)(2,1)}, bf16[4,8,32,128]{3,2,1,0:T(8,128)(2,1)S(1)}, u32[]{:S(2)}) copy-start(bf16[4,8,32,128]{3,2,1,0:T(8,128)(2,1)S(1)} %get-tuple-element.64) | copy-start | bytes 786436
  44.7 1.6 copy-start.40
  44.7 1.9 copy-start.48
  48.8 30.1 %copy-start.78 = (f32[128]{0:T(128)S(1)}, f32[128]{0:T(128)}, u32[]{:S(2)}) copy-start(f32[128]{0:T(128)} %param.11) | copy-start | bytes 1540
  49.2 34.0 %copy-start.57 = (bf16[1,4,4,3,64]{4,2,3,1,0:T(4,128)(2,1)S(1)}, bf16[1,4,4,3,64]{4,2,3,1,0:T(4,128)(2,1)}, u32[]{:S(2)}) copy-start(bf16[1,4,4,3,64]{4,2,3,1,0:T(4,128)(2,1)} %param.13) | copy-start | bytes 18436
  79.4 3.9 %collective-permute-start.3 = (bf16[4,1,32,3]{2,3,1,0:T(4,128)(2,1)S(1)}, bf16[4,1,32,3]{2,3,1,0:T(4,128)(2,1)S(1)}, u32[]{:S(2)}, u32[]{:S(2)}) collective-permute-start(bf16[4,1,32,3]{2,3,1,0:T(4,128)(2,1)S(1)} %get-tuple-element.80), channel_id=1, source_target_pairs={{0,1},{1,2},{2,3},{3,4},{4,5},{5,6},{6,7},{7,8},{8,9},{9,10},{10,1... | collective-permute-start | bytes 2312 | tf_op jit(solution)/shard_map/ppermute | solution.py:261
  81.9 4.4 %collective-permute-start.4 = (bf16[4,1,32,3]{2,3,1,0:T(4,128)(2,1)S(1)}, bf16[4,1,32,3]{2,3,1,0:T(4,128)(2,1)S(1)}, u32[]{:S(2)}, u32[]{:S(2)}) collective-permute-start(bf16[4,1,32,3]{2,3,1,0:T(4,128)(2,1)S(1)} %get-tuple-element.81), channel_id=1, source_target_pairs={{1,0},{2,1},{3,2},{4,3},{5,4},{6,5},{7,6},{8,7},{9,8},{10,9},{11,1... | collective-permute-start | bytes 2312 | tf_op jit(solution)/shard_map/ppermute | solution.py:264
  83.3 33.8 %copy-start.62 = (bf16[1,1,1,3,64]{4,2,3,1,0:T(2,128)(2,1)}, bf16[1,1,1,3,64]{4,2,3,1,0:T(2,128)(2,1)S(1)}, u32[]{:S(2)}) copy-start(bf16[1,1,1,3,64]{4,2,3,1,0:T(2,128)(2,1)S(1)} %get-tuple-element.92) | copy-start | bytes 1156
  83.3 33.8 %copy-start.66 = (bf16[1,1,1,3,64]{4,2,3,1,0:T(2,128)(2,1)}, bf16[1,1,1,3,64]{4,2,3,1,0:T(2,128)(2,1)S(1)}, u32[]{:S(2)}) copy-start(bf16[1,1,1,3,64]{4,2,3,1,0:T(2,128)(2,1)S(1)} %get-tuple-element.93) | copy-start | bytes 1156
  83.3 33.8 %copy-start.68 = (bf16[1,1,1,3,64]{4,2,3,1,0:T(2,128)(2,1)}, bf16[1,1,1,3,64]{4,2,3,1,0:T(2,128)(2,1)S(1)}, u32[]{:S(2)}) copy-start(bf16[1,1,1,3,64]{4,2,3,1,0:T(2,128)(2,1)S(1)} %get-tuple-element.88) | copy-start | bytes 1156
  83.3 33.8 %copy-start.70 = (bf16[1,1,1,3,64]{4,2,3,1,0:T(2,128)(2,1)}, bf16[1,1,1,3,64]{4,2,3,1,0:T(2,128)(2,1)S(1)}, u32[]{:S(2)}) copy-start(bf16[1,1,1,3,64]{4,2,3,1,0:T(2,128)(2,1)S(1)} %get-tuple-element.96) | copy-start | bytes 1156
  83.3 33.8 %copy-start.72 = (bf16[1,1,1,3,64]{4,2,3,1,0:T(2,128)(2,1)}, bf16[1,1,1,3,64]{4,2,3,1,0:T(2,128)(2,1)S(1)}, u32[]{:S(2)}) copy-start(bf16[1,1,1,3,64]{4,2,3,1,0:T(2,128)(2,1)S(1)} %get-tuple-element.89) | copy-start | bytes 1156
  83.3 33.8 %copy-start.74 = (bf16[1,1,1,3,64]{4,2,3,1,0:T(2,128)(2,1)}, bf16[1,1,1,3,64]{4,2,3,1,0:T(2,128)(2,1)S(1)}, u32[]{:S(2)}) copy-start(bf16[1,1,1,3,64]{4,2,3,1,0:T(2,128)(2,1)S(1)} %get-tuple-element.97) | copy-start | bytes 1156
  83.3 34.2 %copy-start.64 = (bf16[1,1,1,3,64]{4,2,3,1,0:T(2,128)(2,1)}, bf16[1,1,1,3,64]{4,2,3,1,0:T(2,128)(2,1)S(1)}, u32[]{:S(2)}) copy-start(bf16[1,1,1,3,64]{4,2,3,1,0:T(2,128)(2,1)S(1)} %get-tuple-element.85) | copy-start | bytes 1156
  83.3 34.4 %copy-start.60 = (bf16[1,1,1,3,64]{4,2,3,1,0:T(2,128)(2,1)}, bf16[1,1,1,3,64]{4,2,3,1,0:T(2,128)(2,1)S(1)}, u32[]{:S(2)}) copy-start(bf16[1,1,1,3,64]{4,2,3,1,0:T(2,128)(2,1)S(1)} %get-tuple-element.84) | copy-start | bytes 1156
  83.4 34.8 %copy-start.58 = (bf16[1,1,1,3,64]{4,2,3,1,0:T(2,128)(2,1)}, bf16[1,1,1,3,64]{4,2,3,1,0:T(2,128)(2,1)S(1)}, u32[]{:S(2)}) copy-start(bf16[1,1,1,3,64]{4,2,3,1,0:T(2,128)(2,1)S(1)} %get-tuple-element.82) | copy-start | bytes 1156
  116.8 17.7 %copy-start.3 = (bf16[2,4,4,64,128]{4,3,2,1,0:T(8,128)(2,1)S(1)}, bf16[2,4,4,64,128]{4,3,2,1,0:T(8,128)(2,1)}, u32[]{:S(2)}) copy-start(bf16[2,4,4,64,128]{4,3,2,1,0:T(8,128)(2,1)} %param.14) | copy-start | bytes 1572868
  118.2 20.3 %copy-start.77 = (f32[1,2,2,8,128]{4,3,2,1,0:T(8,128)S(1)}, f32[1,2,2,8,128]{4,3,2,1,0:T(8,128)}, u32[]{:S(2)}) copy-start(f32[1,2,2,8,128]{4,3,2,1,0:T(8,128)} %param.15) | copy-start | bytes 49156
  118.5 3.5 %collective-permute-start.5 = (bf16[4,1,16,64]{3,2,1,0:T(8,128)(2,1)S(1)}, bf16[4,1,16,64]{3,2,1,0:T(8,128)(2,1)S(1)}, u32[]{:S(2)}, u32[]{:S(2)}) collective-permute-start(bf16[4,1,16,64]{3,2,1,0:T(8,128)(2,1)S(1)} %get-tuple-element.78), channel_id=1, source_target_pairs={{0,1},{1,2},{2,3},{3,4},{4,5},{5,6},{6,7},{7,8},{8,9},{9,10},{10,1... | collective-permute-start | bytes 24584 | tf_op jit(solution)/shard_map/ppermute | solution.py:261
  120.7 8.8 %collective-permute-start.6 = (bf16[4,1,16,64]{3,2,1,0:T(8,128)(2,1)S(1)}, bf16[4,1,16,64]{3,2,1,0:T(8,128)(2,1)S(1)}, u32[]{:S(2)}, u32[]{:S(2)}) collective-permute-start(bf16[4,1,16,64]{3,2,1,0:T(8,128)(2,1)S(1)} %get-tuple-element.79), channel_id=1, source_target_pairs={{1,0},{2,1},{3,2},{4,3},{5,4},{6,5},{7,6},{8,7},{9,8},{10,9},{11,1... | collective-permute-start | bytes 24584 | tf_op jit(solution)/shard_map/ppermute | solution.py:264
  138.7 10.7 %collective-permute-start.7 = (bf16[2,1,8,128]{3,2,1,0:T(8,128)(2,1)S(1)}, bf16[2,1,8,128]{3,2,1,0:T(8,128)(2,1)S(1)}, u32[]{:S(2)}, u32[]{:S(2)}) collective-permute-start(bf16[2,1,8,128]{3,2,1,0:T(8,128)(2,1)S(1)} %get-tuple-element.98), channel_id=1, source_target_pairs={{0,1},{1,2},{2,3},{3,4},{4,5},{5,6},{6,7},{7,8},{8,9},{9,10},{10,1... | collective-permute-start | bytes 12296 | tf_op jit(solution)/shard_map/ppermute | solution.py:261
  148.0 4.4 %collective-permute-start.8 = (bf16[2,1,8,128]{3,2,1,0:T(8,128)(2,1)S(1)}, bf16[2,1,8,128]{3,2,1,0:T(8,128)(2,1)S(1)}, u32[]{:S(2)}, u32[]{:S(2)}) collective-permute-start(bf16[2,1,8,128]{3,2,1,0:T(8,128)(2,1)S(1)} %get-tuple-element.99), channel_id=1, source_target_pairs={{1,0},{2,1},{3,2},{4,3},{5,4},{6,5},{7,6},{8,7},{9,8},{10,9},{11,1... | collective-permute-start | bytes 12296 | tf_op jit(solution)/shard_map/ppermute | solution.py:264
  157.3 16.3 %collective-permute-start.10 = (bf16[4,1,16,64]{3,2,1,0:T(8,128)(2,1)S(1)}, bf16[4,1,16,64]{3,2,1,0:T(8,128)(2,1)S(1)}, u32[]{:S(2)}, u32[]{:S(2)}) collective-permute-start(bf16[4,1,16,64]{3,2,1,0:T(8,128)(2,1)S(1)} %get-tuple-element.77), channel_id=1, source_target_pairs={{1,0},{2,1},{3,2},{4,3},{5,4},{6,5},{7,6},{8,7},{9,8},{10,9},{11,1... | collective-permute-start | bytes 24584 | tf_op jit(solution)/shard_map/ppermute | solution.py:264
  158.7 15.0 %collective-permute-start.9 = (bf16[4,1,16,64]{3,2,1,0:T(8,128)(2,1)S(1)}, bf16[4,1,16,64]{3,2,1,0:T(8,128)(2,1)S(1)}, u32[]{:S(2)}, u32[]{:S(2)}) collective-permute-start(bf16[4,1,16,64]{3,2,1,0:T(8,128)(2,1)S(1)} %get-tuple-element.76), channel_id=1, source_target_pairs={{0,1},{1,2},{2,3},{3,4},{4,5},{5,6},{6,7},{7,8},{8,9},{9,10},{10,1... | collective-permute-start | bytes 24584 | tf_op jit(solution)/shard_map/ppermute | solution.py:261
  167.5 7.5 %copy-start.75 = (bf16[1,1,1,3,64]{4,2,3,1,0:T(2,128)(2,1)S(1)}, bf16[1,1,1,3,64]{4,2,3,1,0:T(2,128)(2,1)}, u32[]{:S(2)}) copy-start(bf16[1,1,1,3,64]{4,2,3,1,0:T(2,128)(2,1)} %copy-done.74) | copy-start | bytes 1156
  167.5 7.8 %copy-start.73 = (bf16[1,1,1,3,64]{4,2,3,1,0:T(2,128)(2,1)S(1)}, bf16[1,1,1,3,64]{4,2,3,1,0:T(2,128)(2,1)}, u32[]{:S(2)}) copy-start(bf16[1,1,1,3,64]{4,2,3,1,0:T(2,128)(2,1)} %copy-done.72) | copy-start | bytes 1156
  168.3 7.8 %copy-start.71 = (bf16[1,1,1,3,64]{4,2,3,1,0:T(2,128)(2,1)S(1)}, bf16[1,1,1,3,64]{4,2,3,1,0:T(2,128)(2,1)}, u32[]{:S(2)}) copy-start(bf16[1,1,1,3,64]{4,2,3,1,0:T(2,128)(2,1)} %copy-done.70) | copy-start | bytes 1156
  169.0 7.3 %copy-start.69 = (bf16[1,1,1,3,64]{4,2,3,1,0:T(2,128)(2,1)S(1)}, bf16[1,1,1,3,64]{4,2,3,1,0:T(2,128)(2,1)}, u32[]{:S(2)}) copy-start(bf16[1,1,1,3,64]{4,2,3,1,0:T(2,128)(2,1)} %copy-done.68) | copy-start | bytes 1156
  170.5 6.5 %copy-start.67 = (bf16[1,1,1,3,64]{4,2,3,1,0:T(2,128)(2,1)S(1)}, bf16[1,1,1,3,64]{4,2,3,1,0:T(2,128)(2,1)}, u32[]{:S(2)}) copy-start(bf16[1,1,1,3,64]{4,2,3,1,0:T(2,128)(2,1)} %copy-done.66) | copy-start | bytes 1156
  171.2 6.1 %copy-start.65 = (bf16[1,1,1,3,64]{4,2,3,1,0:T(2,128)(2,1)S(1)}, bf16[1,1,1,3,64]{4,2,3,1,0:T(2,128)(2,1)}, u32[]{:S(2)}) copy-start(bf16[1,1,1,3,64]{4,2,3,1,0:T(2,128)(2,1)} %copy-done.64) | copy-start | bytes 1156
  172.7 5.3 %copy-start.63 = (bf16[1,1,1,3,64]{4,2,3,1,0:T(2,128)(2,1)S(1)}, bf16[1,1,1,3,64]{4,2,3,1,0:T(2,128)(2,1)}, u32[]{:S(2)}) copy-start(bf16[1,1,1,3,64]{4,2,3,1,0:T(2,128)(2,1)} %copy-done.62) | copy-start | bytes 1156
  173.5 4.9 %copy-start.61 = (bf16[1,1,1,3,64]{4,2,3,1,0:T(2,128)(2,1)S(1)}, bf16[1,1,1,3,64]{4,2,3,1,0:T(2,128)(2,1)}, u32[]{:S(2)}) copy-start(bf16[1,1,1,3,64]{4,2,3,1,0:T(2,128)(2,1)} %copy-done.60) | copy-start | bytes 1156
  173.6 5.1 %copy-start.59 = (bf16[1,1,1,3,64]{4,2,3,1,0:T(2,128)(2,1)S(1)}, bf16[1,1,1,3,64]{4,2,3,1,0:T(2,128)(2,1)}, u32[]{:S(2)}) copy-start(bf16[1,1,1,3,64]{4,2,3,1,0:T(2,128)(2,1)} %copy-done.58) | copy-start | bytes 1156
  177.0 3.4 %copy-start.79 = (f32[128]{0:T(128)S(1)}, f32[128]{0:T(128)}, u32[]{:S(2)}) copy-start(f32[128]{0:T(128)} %param.11) | copy-start | bytes 1540
  180.5 31.3 %copy-start.39 = (bf16[4,8,32,128]{3,2,1,0:T(8,128)(2,1)S(1)}, bf16[4,8,32,128]{3,2,1,0:T(8,128)(2,1)}, u32[]{:S(2)}) copy-start(bf16[4,8,32,128]{3,2,1,0:T(8,128)(2,1)} %copy-done.38) | copy-start | bytes 786436
  180.5 31.3 %copy-start.47 = (bf16[4,8,32,128]{3,2,1,0:T(8,128)(2,1)S(1)}, bf16[4,8,32,128]{3,2,1,0:T(8,128)(2,1)}, u32[]{:S(2)}) copy-start(bf16[4,8,32,128]{3,2,1,0:T(8,128)(2,1)} %copy-done.46) | copy-start | bytes 786436
  211.8 1.5 copy-start.35
  217.7 4.4 %copy-start.11 = (bf16[4,8,32,128]{3,2,1,0:T(8,128)(2,1)S(1)}, bf16[4,8,32,128]{3,2,1,0:T(8,128)(2,1)}, u32[]{:S(2)}) copy-start(bf16[4,8,32,128]{3,2,1,0:T(8,128)(2,1)} %copy-done.10) | copy-start | bytes 786436
  217.7 4.4 %copy-start.13 = (bf16[4,8,32,128]{3,2,1,0:T(8,128)(2,1)S(1)}, bf16[4,8,32,128]{3,2,1,0:T(8,128)(2,1)}, u32[]{:S(2)}) copy-start(bf16[4,8,32,128]{3,2,1,0:T(8,128)(2,1)} %copy-done.12) | copy-start | bytes 786436
  218.1 4.9 %collective-permute-start.11 = (bf16[4,1,32,128]{3,2,1,0:T(8,128)(2,1)S(1)}, bf16[4,1,32,128]{3,2,1,0:T(8,128)(2,1)S(1)}, u32[]{:S(2)}, u32[]{:S(2)}) collective-permute-start(bf16[4,1,32,128]{3,2,1,0:T(8,128)(2,1)S(1)} %get-tuple-element.72), channel_id=1, source_target_pairs={{0,1},{1,2},{2,3},{3,4},{4,5},{5,6},{6,7},{7,8},{8,9},{9,10},{10,1... | collective-permute-start | bytes 98312 | tf_op jit(solution)/shard_map/ppermute | solution.py:261
  220.7 1.9 copy-start.7
  220.7 1.9 copy-start.9
  220.7 4.8 %collective-permute-start.12 = (bf16[4,1,32,128]{3,2,1,0:T(8,128)(2,1)S(1)}, bf16[4,1,32,128]{3,2,1,0:T(8,128)(2,1)S(1)}, u32[]{:S(2)}, u32[]{:S(2)}) collective-permute-start(bf16[4,1,32,128]{3,2,1,0:T(8,128)(2,1)S(1)} %get-tuple-element.73), channel_id=1, source_target_pairs={{1,0},{2,1},{3,2},{4,3},{5,4},{6,5},{7,6},{8,7},{9,8},{10,9},{11,1... | collective-permute-start | bytes 98312 | tf_op jit(solution)/shard_map/ppermute | solution.py:264
  222.6 4.4 %copy-start.5 = (bf16[4,8,32,128]{3,2,1,0:T(8,128)(2,1)S(1)}, bf16[4,8,32,128]{3,2,1,0:T(8,128)(2,1)}, u32[]{:S(2)}) copy-start(bf16[4,8,32,128]{3,2,1,0:T(8,128)(2,1)} %copy-done.4) | copy-start | bytes 786436
  225.5 70.8 %collective-permute-start.13 = (bf16[2,10,32,128]{3,2,1,0:T(8,128)(2,1)S(1)}, bf16[2,10,32,128]{3,2,1,0:T(8,128)(2,1)S(1)}, u32[]{:S(2)}, u32[]{:S(2)}) collective-permute-start(bf16[2,10,32,128]{3,2,1,0:T(8,128)(2,1)S(1)} %pad_maximum_fusion.29), channel_id=1, source_target_pairs={{16,0},{32,16},{48,32},{17,1},{33,17},{49,33},{18,2},{34,18},{50,3... | collective-permute-start | bytes 491528 | tf_op jit(solution)/shard_map/ppermute | solution.py:272
  (30 other events, 30.4 us)

commit v2 on v0

v2 whole, which is shorter than its diff:
```python
import jax
import jax.numpy as jnp
import numpy as np
from jax import lax
from jax.experimental import pallas as pl
from jax.experimental.pallas import tpu as pltpu
from jax.sharding import PartitionSpec as P

EPSILON = 1e-06
LOW = jnp.bfloat16
WIDE = jnp.float32
LOCAL = 1024
PER_CLIP = 64


def group_total(values):
    lane = lax.broadcasted_iota(jnp.int32, values.shape, 1)
    paired = values + jnp.where(
        lane % 2 == 0, pltpu.roll(values, 127, 1), pltpu.roll(values, 1, 1)
    )
    return paired + jnp.where(
        lane % 4 < 2, pltpu.roll(paired, 126, 1), pltpu.roll(paired, 2, 1)
    )


def tile(row):
    return jnp.broadcast_to(row, (8, row.shape[-1]))


def silu_slope(values):
    logistic = jax.nn.sigmoid(values)
    return logistic * (1.0 + values * (1.0 - logistic))


def place():
    batch = lax.axis_index("batch")
    row = lax.axis_index("row")
    return dict(
        batch=batch,
        z_lo=batch // 2,
        core=batch % 2,
        frame=lax.axis_index("frame"),
        row=row,
        z_hi=row // 4,
        y=row % 4,
    )


def device(me, **changed):
    at = dict(me, **changed)
    return (at["z_lo"] * 2 + at["core"], at["frame"], at["z_hi"] * 4 + at["y"])


def neighbour(me, frame_step, row_step):
    return (me["batch"], (me["frame"] + frame_step) % 4, (me["row"] + row_step) % 16)


def plane_peers(me):
    own = me["frame"] * 4 + me["y"]
    others = [(own + step) % 16 for step in range(1, 16)]
    return [(other, device(me, frame=other // 4, y=other % 4)) for other in others]


def z_peers(me):
    own = me["z_hi"] * 4 + me["z_lo"]
    others = [(own + step) % 16 for step in range(1, 16)]
    return [(other, device(me, z_hi=other // 4, z_lo=other % 4)) for other in others]


def high_peers(me):
    others = [(me["z_hi"] + step) % 4 for step in range(1, 4)]
    return [(other, device(me, z_hi=other)) for other in others]


def push(src, dst, peer, send_sem, recv_sem):
    pltpu.make_async_remote_copy(
        src_ref=src,
        dst_ref=dst,
        send_sem=send_sem,
        recv_sem=recv_sem,
        device_id=peer,
        device_id_type=pl.DeviceIdType.MESH,
    ).start()


def arrived(like, sem):
    pltpu.make_async_copy(like, like, sem).wait()


def selections():
    rows_first = np.zeros((160, 96), np.float32)
    for k in range(4):
        for a in range(10):
            for t in range(4):
                block, r = divmod(2 * a + k + 1, 8)
                rows_first[k * 40 + a * 4 + t, block * 32 + t * 8 + r] = 1
    rows_second = np.zeros((64, 40), np.float32)
    for m in range(2):
        for k in range(4):
            for u in range(2):
                for b in range(4):
                    rows_second[(m * 4 + k) * 8 + u * 4 + b, (2 * b + k) * 4 + 2 * u + m] = 1
    rows_back = np.zeros((32, 96), np.float32)
    for k in range(4):
        for a in range(2, 8):
            for t in range(4):
                r = 2 * a + k - 7
                if 0 <= r < 8:
                    rows_back[t * 8 + r, k * 24 + (a - 2) * 4 + t] = 1
    return (
        jnp.asarray(rows_first, LOW),
        jnp.asarray(rows_second, LOW),
        jnp.asarray(rows_second.T[8:32].copy(), WIDE),
        jnp.asarray(rows_back, WIDE),
    )


def column_sum(left, middle, right):
    column = lax.broadcasted_iota(jnp.int32, middle.shape, 0) % 32
    rows = middle.shape[0]
    return (
        middle
        + jnp.where(column == 0, 0.0, pltpu.roll(left, 1, 0))
        + jnp.where(column == 31, 0.0, pltpu.roll(right, rows - 1, 0))
    )


def across(left, right):
    return lax.dot_general(left, right, (((1,), (1,)), ((), ())), preferred_element_type=WIDE)


def wide_dot(left, right):
    return jnp.dot(left, right, preferred_element_type=WIDE)


def exact_pick(pick, values):
    return jnp.dot(pick, values, precision=lax.Precision.HIGHEST, preferred_element_type=WIDE)


def step_kernel(
    x_ref, gain1_ref, w_ref, gain2_ref, ow_ref, d1_ref, d2_ref, score_ref,
    pick_first, pick_second, pick_second_back, pick_first_back,
    out_ref, upd_ref,
    xe, ae, ge, mx, ag, wg, xt, g3, w_fwd, w_back,
    ow_f, ow_cols, ow_rows, d1_f, d1_rows, images, sg, sg_flat,
    dw, pair_out, pair_in, plane_out, plane_in, z_out, z_in, z_all, gathered,
    plane, high, stat_send, stat_recv, halo_send, halo_recv, sum_send, sum_recv,
):
    me = place()
    frame, row, core, y, z_hi = (me["frame"], me["row"], me["core"], me["y"], me["z_hi"])
    z = z_hi * 4 + me["z_lo"]
    slot = frame * 4 + y
    plane_line, z_line, high_line = (plane_peers(me), z_peers(me), high_peers(me))
    partner = device(me, core=1 - core)
    above, below = (neighbour(me, 0, -1), neighbour(me, 0, 1))
    corners = [neighbour(me, f, r) for f in (-1, 1) for r in (-1, 1)]

    barrier = pltpu.get_barrier_semaphore()
    greeted = [p for _, p in z_line] + [above, below] + corners
    greeted += [p for _, p in plane_line] + [partner]
    for peer in greeted:
        pl.semaphore_signal(
            barrier, inc=1, device_id=peer, device_id_type=pl.DeviceIdType.MESH
        )

    def plane_start(turn, first, second):
        plane[turn, slot, 0:1, :] = first
        plane[turn, slot, 1:2, :] = second
        for _, peer in plane_line:
            push(plane.at[turn, slot], plane.at[turn, slot], peer, stat_send.at[turn, 0], stat_recv.at[turn, 0])

    def plane_wait(turn):
        others = plane.at[turn, pl.ds(0, 15)]
        arrived(others, stat_recv.at[turn, 0])
        arrived(others, stat_send.at[turn, 0])

    def high_start(turn, first, second):
        high[turn, z_hi, 0:1, :] = first
        high[turn, z_hi, 1:2, :] = second
        for _, peer in high_line:
            push(high.at[turn, z_hi], high.at[turn, z_hi], peer, stat_send.at[turn, 1], stat_recv.at[turn, 1])

    def high_wait(turn):
        others = high.at[turn, pl.ds(0, 3)]
        arrived(others, stat_recv.at[turn, 1])
        arrived(others, stat_send.at[turn, 1])

    def moments_middle(turn):
        plane_wait(turn)
        means, squares = (plane[turn, :, 0, :], plane[turn, :, 1, :])
        mean = group_total(tile(jnp.sum(means, axis=0, keepdims=True))) / 64.0
        apart = means - mean[0:1]
        total = jnp.sum(squares + float(LOCAL) * (apart * apart), axis=0, keepdims=True)
        high_start(turn, mean[0:1], group_total(tile(total))[0:1])

    def moments_end(turn):
        high_wait(turn)
        means, squares = (high[turn, :, 0, :], high[turn, :, 1, :])
        mean = jnp.sum(means, axis=0, keepdims=True) / 4.0
        apart = means - mean
        total = jnp.sum(squares + (64.0 * LOCAL) * (apart * apart), axis=0, keepdims=True)
        return (mean, lax.rsqrt(total / (4.0 * LOCAL * PER_CLIP) + EPSILON))

    def sums_middle(turn):
        plane_wait(turn)
        sums = jnp.sum(plane[turn], axis=0)
        high_start(turn, group_total(tile(sums[0:1]))[0:1], group_total(tile(sums[1:2]))[0:1])

    def sums_end(turn):
        high_wait(turn)
        means = jnp.sum(high[turn], axis=0) / (4.0 * LOCAL * PER_CLIP)
        return (means[0:1], means[1:2])

    def local_moments(read):
        zero = jnp.zeros((1, 128), WIDE)
        total = lax.fori_loop(
            0, 4, lambda t, acc: acc + jnp.sum(read(t), axis=0, keepdims=True), zero
        )
        mean = total / float(LOCAL)

        def squares(t, acc):
            apart = read(t) - mean
            return acc + jnp.sum(apart * apart, axis=0, keepdims=True)

        return (mean, lax.fori_loop(0, 4, squares, zero))

    def halo_start(turn, src, dst, own_row, own_frames, to_frames, frame_step):
        def go(index, source, target, peer):
            push(source, target, peer, halo_send.at[turn, index], halo_recv.at[turn, index])

        inner = pl.ds(own_frames[0], 4)
        edge = pl.ds(own_frames[1], 2)
        base = pl.ds(own_frames[2], 4)
        far = pl.ds(to_frames, 2)
        go(0, src.at[inner, own_row + 7], dst.at[base, 0], below)
        go(1, src.at[inner, own_row], dst.at[base, 9], above)
        go(2, src.at[edge, pl.ds(own_row, 8)], dst.at[far, pl.ds(1, 8)], neighbour(me, frame_step, 0))
        go(3, src.at[edge, own_row + 7], dst.at[far, 0], neighbour(me, frame_step, 1))
        go(4, src.at[edge, own_row], dst.at[far, 9], neighbour(me, frame_step, -1))

    def halo_wait(turn, dst, base_frame, to_frames):
        base = pl.ds(base_frame, 4)
        far = pl.ds(to_frames, 2)
        parts = [
            dst.at[base, 0],
            dst.at[base, 9],
            dst.at[far, pl.ds(1, 8)],
            dst.at[far, 0],
            dst.at[far, 9],
        ]
        for index, part in enumerate(parts):
            arrived(part, halo_recv.at[turn, index])
            arrived(part, halo_send.at[turn, index])

    def inside(shape, outside_frame):
        position = lax.broadcasted_iota(jnp.int32, shape, 0)
        low = jnp.where(row == 0, 32, 0)
        high_end = jnp.where(row == 15, 288, 320)
        high_end = jnp.where(outside_frame, 0, high_end)
        return (position >= low) & (position < high_end)

    def own_input(t):
        return x_ref[t].astype(WIDE).reshape(256, 128)

    mean, squares = local_moments(own_input)
    xe[2:6, 1:9] = x_ref[...]
    sg[:, 1:3] = score_ref[...]
    pl.semaphore_wait(barrier, len(greeted))
    plane_start(0, mean, squares)
    halo_start(0, x_ref, xe, 0, (0, 2, 2), 0, 1)
    push(score_ref.at[:, 1], sg.at[:, 0], below, halo_send.at[0, 5], halo_recv.at[0, 5])
    push(score_ref.at[:, 0], sg.at[:, 3], above, halo_send.at[0, 6], halo_recv.at[0, 6])

    @pl.loop(0, 9)
    def _(tap):
        for c in range(3):
            w_fwd[pl.ds(tap * 128, 128), c * 128 : (c + 1) * 128] = w_ref[tap * 3 + c]

    moments_middle(0)

    ow_f[...] = jnp.zeros((128, 128), WIDE)
    ow_f[:, 0:3] = ow_ref[...].astype(WIDE)
    colours = ow_f[...]
    colours_t = colours.T
    for c in range(32):
        ow_cols[c * 128 : (c + 1) * 128, :] = (
            colours if c == 0 else pltpu.roll(colours, 3 * c, 1)
        ).astype(LOW)
        ow_rows[:, c * 128 : (c + 1) * 128] = (
            colours_t if c == 0 else pltpu.roll(colours_t, 3 * c, 0)
        ).astype(LOW)
    for k in range(4):
        d1_f[...] = jnp.zeros((128, 128), WIDE)
        for l in range(4):
            d1_f[3 * l : 3 * l + 3, 0:64] = d1_ref[k * 4 + l].astype(WIDE)
        single = d1_f[...]
        double = single + pltpu.roll(pltpu.roll(single, 64, 1), 6, 0)
        for p in range(8):
            d1_rows[k * 128 : (k + 1) * 128, p * 128 : (p + 1) * 128] = pltpu.roll(
                double, (12 * p - 3) % 128, 0
            ).astype(LOW)

    @pl.loop(0, 9)
    def _(tap):
        for c in range(3):
            w_back[pl.ds(tap * 128, 128), c * 128 : (c + 1) * 128] = (
                w_ref[tap * 3 + c].astype(WIDE).T.astype(LOW)
            )

    halo_wait(0, xe, 2, 0)
    for index in (5, 6):
        arrived(sg.at[:, 0], halo_recv.at[0, index])
        arrived(sg.at[:, 0], halo_send.at[0, index])
    gain1 = gain1_ref[...]
    gain2 = gain2_ref[...]
    mean1, inverse1 = moments_end(0)

    @pl.loop(0, 6)
    def _(t):
        scaled = (xe[t].astype(WIDE).reshape(320, 128) - mean1) * inverse1 * gain1
        act = scaled * jax.nn.sigmoid(scaled)
        keep = inside(act.shape, (t < 2) & (frame == 0))
        ae[t] = jnp.where(keep, act, 0.0).astype(LOW).reshape(10, 32, 128)

    @pl.loop(0, 4)
    def _(t):
        taps = [ae[t + i, j : j + 8].reshape(256, 128) for i in range(3) for j in range(3)]
        product = wide_dot(jnp.concatenate(taps, axis=1), w_fwd[...])
        branch = column_sum(product[:, 0:128], product[:, 128:256], product[:, 256:384])
        mx[t] = (xe[t + 2, 1:9].astype(WIDE).reshape(256, 128) + branch).astype(LOW)

    mean, squares = local_moments(lambda t: mx[t].astype(WIDE))
    plane_start(1, mean, squares)

    @pl.loop(0, 6)
    def _(t):
        for j in range(3):
            xt[j, t] = ae[t, j : j + 8].reshape(256, 128).astype(WIDE).T.astype(LOW)

    moments_middle(1)
    mean2, inverse2 = moments_end(1)

    def normed_second(t):
        return (mx[t].astype(WIDE) - mean2) * inverse2

    @pl.loop(0, 4)
    def _(t):
        scaled = normed_second(t) * gain2
        act = (scaled * jax.nn.sigmoid(scaled)).astype(LOW)
        ag[pl.ds(t * 256, 256), :] = act.astype(WIDE)

    image = jnp.zeros((32, 128), WIDE)
    for part in range(4):
        columns = [ag[pl.ds(c, 32, stride=32), :] for c in range(part * 8, part * 8 + 8)]
        image = image + wide_dot(
            jnp.concatenate(columns, axis=1).astype(LOW), ow_cols[part * 1024 : (part + 1) * 1024, :]
        )
    images[1] = image.astype(LOW)
    push(images.at[1], images.at[0], below, halo_send.at[1, 5], halo_recv.at[1, 5])
    push(images.at[1], images.at[2], above, halo_send.at[1, 6], halo_recv.at[1, 6])
    sg_flat[...] = sg[...].reshape(64, 128)
    score = jnp.concatenate([sg_flat[pl.ds(p, 8, stride=8), :] for p in range(8)], axis=0)
    for index in (5, 6):
        arrived(images.at[0], halo_recv.at[1, index])
        arrived(images.at[0], halo_send.at[1, index])

    strips = jnp.concatenate(
        [
            jnp.where(row == 0, 0.0, images[0].astype(WIDE)),
            images[1].astype(WIDE),
            jnp.where(row == 15, 0.0, images[2].astype(WIDE)),
        ],
        axis=0,
    ).astype(LOW)
    picked = wide_dot(pick_first[...], strips)
    taps = [picked[k * 40 : (k + 1) * 40] for k in range(4)]
    first_pre = wide_dot(jnp.concatenate(taps, axis=1).astype(LOW), d1_rows[...])
    place_row = lax.broadcasted_iota(jnp.int32, first_pre.shape, 0)
    low_row = jnp.where(row == 0, 12, 0)
    high_row = jnp.where(row == 15, 28, 40)
    real = (place_row >= low_row) & (place_row < high_row)
    first_act = jnp.where(real, first_pre * jax.nn.sigmoid(first_pre), 0.0).astype(LOW)
    picked = wide_dot(pick_second[...], first_act)
    blank = jnp.zeros((8, 128), WIDE)
    lane = lax.broadcasted_iota(jnp.int32, (64, 128), 1)
    second_pre = jnp.zeros((64, 128), WIDE)
    for tap in range(8):
        middle = jnp.concatenate(
            [picked[tap * 8 : tap * 8 + 8, p * 128 : (p + 1) * 128] for p in range(8)], axis=0
        )
        turned = pltpu.roll(middle, 64, 1)
        sides = jnp.where(
            lane < 64,
            jnp.concatenate([blank, turned[0:56]], axis=0),
            jnp.concatenate([turned[8:64], blank], axis=0),
        )
        weights = jnp.concatenate([d2_ref[tap * 4 + l] for l in (1, 2, 0, 3)], axis=0)
        second_pre = second_pre + wide_dot(
            jnp.concatenate([middle, sides], axis=1).astype(LOW), weights
        )
    strip = lax.broadcasted_iota(jnp.int32, (64, 128), 0) % 4
    first_strip = jnp.where(row == 0, 1, 0)
    last_strip = jnp.where(row == 15, 2, 3)
    score_pre = jnp.where(
        (strip >= first_strip) & (strip <= last_strip), score * silu_slope(second_pre), 0.0
    ).astype(LOW).astype(WIDE)
    sources = jnp.concatenate(
        [
            score_pre,
            jnp.concatenate([blank, score_pre[0:56]], axis=0),
            jnp.concatenate([score_pre[8:64], blank], axis=0),
        ],
        axis=1,
    ).astype(LOW)
    nothing = jnp.zeros((64, 128), LOW)
    spread = []
    for tap in range(8):
        even = jnp.concatenate([d2_ref[tap * 4 + 1], d2_ref[tap * 4 + 3], nothing], axis=1)
        odd = jnp.concatenate([d2_ref[tap * 4 + 2], nothing, d2_ref[tap * 4]], axis=1)
        back = across(sources, jnp.concatenate([even, odd], axis=0))
        spread.append(
            jnp.concatenate([back[p * 8 : (p + 1) * 8] for p in range(8)], axis=1)
        )
    first_full = exact_pick(pick_second_back[...], jnp.concatenate(spread, axis=0))
    first_grad = jnp.where(real[8:32], first_full * silu_slope(first_pre[8:32]), 0.0).astype(LOW)
    back = across(first_grad, d1_rows[...])
    stacked = jnp.concatenate([back[:, k * 128 : (k + 1) * 128] for k in range(4)], axis=0)
    image_grad = exact_pick(pick_first_back[...], stacked).astype(LOW)
    for part in range(4):
        grads = wide_dot(image_grad, ow_rows[:, part * 1024 : (part + 1) * 1024])
        for c in range(8):
            ag[pl.ds(part * 8 + c, 32, stride=32), :] = grads[:, c * 128 : (c + 1) * 128]

    def weigh(t, acc):
        normed = normed_second(t)
        here = pl.ds(t * 256, 256)
        weighted = ag[here, :] * silu_slope(normed * gain2) * gain2
        ag[here, :] = weighted
        return (
            acc[0] + jnp.sum(weighted, axis=0, keepdims=True),
            acc[1] + jnp.sum(weighted * normed, axis=0, keepdims=True),
        )

    zeros = (jnp.zeros((1, 128), WIDE), jnp.zeros((1, 128), WIDE))
    sums = lax.fori_loop(0, 4, weigh, zeros)
    plane_start(2, *sums)
    sums_middle(2)
    first_mean, second_mean = sums_end(2)

    @pl.loop(0, 4)
    def _(t):
        here = pl.ds(t * 256, 256)
        grad = (ag[here, :] - first_mean - normed_second(t) * second_mean) * inverse2
        ag[here, :] = grad
        low = grad.astype(LOW)
        ge[t, 1:9] = low.reshape(8, 32, 128)
        grad = low.astype(WIDE)
        column = lax.broadcasted_iota(jnp.int32, grad.shape, 0) % 32
        g3[here, 128:256] = low
        g3[here, 0:128] = jnp.where(column == 31, 0.0, pltpu.roll(grad, 255, 0)).astype(LOW)
        g3[here, 256:384] = jnp.where(column == 0, 0.0, pltpu.roll(grad, 1, 0)).astype(LOW)

    halo_start(1, ge, ge, 1, (0, 0, 0), 4, -1)

    for i in range(3):
        for j in range(3):
            acts = jnp.concatenate([xt[j, i + t] for t in range(4)], axis=1)
            product = wide_dot(acts, g3[...])
            for c in range(3):
                first = ((i * 3 + j) * 3 + c) * 128
                dw[first : first + 128, :] = product[:, c * 128 : (c + 1) * 128]
    dw[3456:3520, :] = jnp.zeros((64, 128), WIDE)
    theirs = pl.ds(pl.multiple_of((1 - core) * 1728, 64), 1792)
    ours = pl.ds(pl.multiple_of(core * 1728, 64), 1792)
    pair_out[...] = dw[theirs, :].astype(LOW)
    push(pair_out, pair_in, partner, sum_send.at[0], sum_recv.at[0])

    halo_wait(1, ge, 0, 4)

    def normed_first(t):
        return (own_input(t) - mean1) * inverse1

    def back_step(t, acc):
        taps = []
        for i in range(3):
            for j in range(3):
                strip = ge[t + 2 - i, 2 - j : 10 - j].reshape(256, 128)
                above_edge = (row == 0) if j == 2 else False
                below_edge = (row == 15) if j == 0 else False
                late = (frame == 3) & (t + 2 - i > 3)
                position = lax.broadcasted_iota(jnp.int32, (256, 128), 0)
                low = jnp.where(above_edge, 32, 0)
                end = jnp.where(late, 0, jnp.where(below_edge, 224, 256))
                keep = (position >= low) & (position < end)
                taps.append(jnp.where(keep, strip.astype(WIDE), 0.0).astype(LOW))
        product = wide_dot(jnp.concatenate(taps, axis=1), w_back[...])
        grad = column_sum(product[:, 256:384], product[:, 128:256], product[:, 0:128])
        normed = normed_first(t)
        weighted = grad * silu_slope(normed * gain1) * gain1
        wg[t] = weighted
        return (
            acc[0] + jnp.sum(weighted, axis=0, keepdims=True),
            acc[1] + jnp.sum(weighted * normed, axis=0, keepdims=True),
        )

    sums = lax.fori_loop(0, 4, back_step, zeros)
    plane_start(3, *sums)

    arrived(pair_in, sum_recv.at[0])
    arrived(pair_in, sum_send.at[0])
    plane_out[...] = (dw[ours, :] + pair_in[...].astype(WIDE)).astype(LOW).reshape(16, 112, 128)
    for other, peer in plane_line:
        push(plane_out.at[other], plane_in.at[slot], peer, sum_send.at[1], sum_recv.at[1])
    plane_in[slot] = plane_out[slot]

    sums_middle(3)

    arrived(plane_in.at[pl.ds(0, 15)], sum_recv.at[1])
    arrived(plane_in.at[pl.ds(0, 15)], sum_send.at[1])
    z_out[0:14] = jnp.sum(plane_in[...].astype(WIDE), axis=0).reshape(14, 8, 128)
    z_out[14:16] = jnp.zeros((2, 8, 128), WIDE)
    for other, peer in z_line:
        push(z_out.at[other], z_in.at[z], peer, sum_send.at[2], sum_recv.at[2])
    z_in[z] = z_out[z]

    first_mean, second_mean = sums_end(3)

    @pl.loop(0, 4)
    def _(t):
        grad = (wg[t] - first_mean - normed_first(t) * second_mean) * inverse1
        out_ref[t] = (ag[pl.ds(t * 256, 256), :] + grad).astype(LOW).reshape(8, 32, 128)

    arrived(z_in.at[pl.ds(0, 15)], sum_recv.at[2])
    arrived(z_in.at[pl.ds(0, 15)], sum_send.at[2])
    z_all[z] = jnp.sum(z_in[...], axis=0)
    for _, peer in z_line:
        push(z_all.at[z], z_all.at[z], peer, sum_send.at[3], sum_recv.at[3])
    arrived(z_all.at[pl.ds(0, 15)], sum_recv.at[3])
    arrived(z_all.at[pl.ds(0, 15)], sum_send.at[3])
    half = gathered.at[core]
    half[slot] = z_all[0:14].reshape(112, 128).astype(LOW)
    for _, peer in plane_line:
        push(half.at[slot], half.at[slot], peer, sum_send.at[4], sum_recv.at[4])
    arrived(half.at[pl.ds(0, 15)], sum_recv.at[4])
    arrived(half.at[pl.ds(0, 15)], sum_send.at[4])
    push(half, half, partner, sum_send.at[5], sum_recv.at[5])
    arrived(half, sum_recv.at[5])
    arrived(half, sum_send.at[5])

    def square(part, acc):
        for core_part in range(2):
            piece = gathered[core_part, part].astype(WIDE)
            piece = jnp.where(
                lax.broadcasted_iota(jnp.int32, piece.shape, 0) + part * 112 < 1728, piece, 0.0
            )
            acc = acc + jnp.sum((piece * piece).reshape(14, 8, 128), axis=0)
        return acc

    total = lax.fori_loop(0, 16, square, jnp.zeros((8, 128), WIDE))
    scale = lax.rsqrt(jnp.sum(total, keepdims=True) / (3456.0 * 128.0) + EPSILON)

    @pl.loop(0, 15)
    def _(part):
        for core_part in range(2):
            upd_ref[core_part, pl.ds(part * 112, 112), :] = gathered[core_part, part].astype(WIDE) * scale

    for core_part in range(2):
        upd_ref[core_part, 1680:1728, :] = gathered[core_part, 15, 0:48].astype(WIDE) * scale


def shards(
    block_input, gain_first, conv_weight, gain_second, out_weight, disc_first, disc_second, score_grad
):
    vmem = pl.BlockSpec(memory_space=pltpu.VMEM)
    low = lambda *shape: pltpu.VMEM(shape, LOW)
    wide = lambda *shape: pltpu.VMEM(shape, WIDE)
    dma = pltpu.SemaphoreType.DMA
    picks = selections()
    input_grad, update = pl.pallas_call(
        step_kernel,
        out_shape=(
            jax.ShapeDtypeStruct((4, 8, 32, 128), LOW),
            jax.ShapeDtypeStruct((2, 1728, 128), WIDE),
        ),
        in_specs=[vmem] * 12,
        out_specs=(vmem, vmem),
        scratch_shapes=[
            low(6, 10, 32, 128), low(6, 10, 32, 128), low(6, 10, 32, 128),
            low(4, 256, 128), wide(1024, 128), wide(4, 256, 128),
            low(3, 6, 128, 256), low(1024, 384), low(1152, 384), low(1152, 384),
            wide(128, 128), low(4096, 128), low(128, 4096), wide(128, 128), low(512, 1024),
            low(3, 32, 128), wide(2, 4, 8, 128), wide(64, 128),
            wide(3520, 128), low(1792, 128), low(1792, 128), low(16, 112, 128), low(16, 112, 128),
            wide(16, 8, 128), wide(16, 8, 128), wide(16, 8, 128), low(2, 16, 112, 128),
            wide(4, 16, 2, 128), wide(4, 4, 2, 128),
            dma((4, 2)), dma((4, 2)), dma((2, 7)), dma((2, 7)), dma((6,)), dma((6,)),
        ],
        compiler_params=pltpu.CompilerParams(
            collective_id=1, has_side_effects=True, vmem_limit_bytes=48 * 1024 * 1024
        ),
    )(
        block_input[0],
        gain_first.reshape(1, 128),
        conv_weight.reshape(27, 128, 128),
        gain_second.reshape(1, 128),
        out_weight,
        disc_first.reshape(16, 3, 64),
        disc_second.reshape(32, 64, 128),
        score_grad[0],
        *picks,
    )
    return (input_grad[None], update.reshape(conv_weight.shape))


def solution(mesh):
    split = P("batch", "frame", "row", None, None)
    in_specs = (split, P(), P(), P(), P(), P(), P(), split)
    return jax.shard_map(
        shards, mesh=mesh, in_specs=in_specs, out_specs=(split, P()), check_vma=False
    )
```

time: 1730 us -> 121 us (0.07)
  blocking collectives: 1150 us -> 0 us
  waiting for transfers between devices: 431 us -> 0 us
  Pallas kernels: 0 us -> 109 us
  local copies, waits for them, and re-layouts: 59.7 us -> 11.5 us
  matrix products: 31.4 us -> 0 us
  starting transfers between devices: 28.7 us -> 0 us
    psum x6 -> x0, blocking collectives: 1150 us -> none  [the longest x2 393 us: norm_forward(): totals = lax.psum(group_sums(values, groups), ('frame', 'row'))]
    psum x1 -> x0, waiting for transfers between devices: 410 us -> none  [shards(): summed_weight = lax.psum(local_weight, ('batch', 'frame', 'row'))]
    pallas_call x0 -> x1, Pallas kernels: none -> 109 us  [shards(): pl.pallas_call(step_kernel, out_shape=(jax.ShapeDtypeStruct((4, 8, 32, 12...]
    slice x71 -> x0, local copies, waits for them, and re-layouts: 47.5 us -> none  [the longest x48 38.6 us: strided_conv(): extended[tap_t::time_taps, tap_r:tap_r + 2 * rows_out:2, tap_c:tap_c + 2...]
    dot_general x125 -> x0, matrix products: 31.4 us -> none  [the longest x48 10.3 us: strided_conv(): jnp.dot(source, weight[tap_t, tap_r, tap_c], preferred_element_type=jnp.f...]
    ppermute x14 -> x0, starting transfers between devices: 28.7 us -> none  [the longest x6 18 us: with_halo(): lax.ppermute(lax.slice_in_dim(block, block.shape[dim] - width, None, axis...]
    ppermute x14 -> x0, waiting for transfers between devices: 20.5 us -> none  [the longest x6 15.4 us: with_halo(): lax.ppermute(lax.slice_in_dim(block, 0, width, axis=dim), axis, backward)]
  transfers between devices with their start and end apart: 15 -> 0, of which waited for: 8 -> 0; matrix products, arithmetic and copies ran while one was open for 1% -> 0% of each run, Pallas kernels for 0% -> 0%
where the time goes in v2:
time: 121 us
  Pallas kernels  109 us (90%)
  local copies, waits for them, and re-layouts  11.5 us (10%)
    pallas_call x1, Pallas kernels, shards(): pl.pallas_call(step_kernel, out_shape=(jax.ShapeDtypeStruct((4, 8, 32, 12...  109 us
    unnamed x24, local copies, waits for them, and re-layouts  11.5 us

profile of v2, /device:TPU:1, one launch (start us, length us, event | category | flops | bytes accessed | tf_op | source)
XLA Modules:
  0.0 120.9 jit_solution(8649749705802051025)
XLA Ops:
  0.6 0.7 copy.14
  1.3 0.8 copy.15.ow_ref
  2.2 0.0 copy-start
  2.2 1.2 copy-done
  3.3 0.0 copy-start.1
  3.3 1.0 copy-done.1
  4.4 0.0 copy-start.2
  4.4 0.9 copy-done.2
  5.3 0.0 copy-start.3
  5.3 0.8 copy-done.3
  6.1 0.0 copy-start.4
  6.1 0.7 copy-done.4
  6.8 0.0 copy-start.5
  6.8 0.7 copy-done.5
  7.5 0.0 copy-start.6
  7.5 0.7 copy-done.6
  8.3 0.0 copy-start.7
  8.3 0.7 copy-done.7
  9.0 0.0 copy-start.8
  9.0 0.7 copy-done.8
  9.6 0.0 copy-start.9
  9.6 0.7 copy-done.9
  10.3 108.7 %shard_map.131 = (bf16[4,8,32,128]{3,2,1,0:T(8,128)(2,1)S(1)}, f32[2,1728,128]{2,1,0:T(8,128)S(1)}) custom-call(bf16[4,8,32,128]{3,2,1,0:T(8,128)(2,1)S(1)} %bitcast.12, f32[1,128]{1,0:T(1,128)S(1)} %bitcast.16, bf16[27,128,128]{2,1,0:T(8,128)(2,1)S(1)} %bitcast.10, f32[1,128]{1,0:T(1,128)S(1)} %bitcast.17, bf16[128,3]{1,0:T(8,128)(2,1)S(1)} %copy.15.ow_ref, ...), custom_call_target="tpu_custom_call" | custom-call | tf_op jit(solution)/shard_map/pallas_call | solution.py:579
  119.0 0.7 copy.18
  119.7 1.2 copy.19
Async XLA Ops:
  2.2 1.2 copy-start
  3.3 1.0 copy-start.1
  4.4 0.9 copy-start.2
  5.3 0.8 copy-start.3
  6.1 0.7 copy-start.4
  6.8 0.7 copy-start.5
  7.5 0.7 copy-start.6
  8.3 0.7 copy-start.7
  9.0 0.7 copy-start.8
  9.6 0.7 copy-start.9

commit v3 on v2

--- a/solution.py
+++ b/solution.py
@@ -65,6 +65,21 @@
     own = me["z_hi"] * 4 + me["z_lo"]
     others = [(own + step) % 16 for step in range(1, 16)]
     return [(other, device(me, z_hi=other // 4, z_lo=other % 4)) for other in others]
+
+
+def clip_peers(me):
+    return [
+        device(
+            me,
+            z_hi=(me["z_hi"] + dz) % 4,
+            y=(me["y"] + dy) % 4,
+            frame=(me["frame"] + dx) % 4,
+        )
+        for dz in (2, 1, 3, 0)
+        for dy in (2, 1, 3, 0)
+        for dx in (2, 1, 3, 0)
+        if (dz, dy, dx) != (0, 0, 0)
+    ]
 
 
 def high_peers(me):
@@ -138,78 +153,107 @@
 
 
 def step_kernel(
-    x_ref, gain1_ref, w_ref, gain2_ref, ow_ref, d1_ref, d2_ref, score_ref,
+    x_hbm, gain1_hbm, w_hbm, gain2_hbm, ow_hbm, d1_hbm, d2_hbm, score_hbm,
+    pick_first_hbm, pick_second_hbm, pick_second_back_hbm, pick_first_back_hbm,
+    out_ref, summed_ref, scale_ref,
+    gain1_ref, w_ref, gain2_ref, ow_ref, d1_ref, d2_ref,
     pick_first, pick_second, pick_second_back, pick_first_back,
-    out_ref, upd_ref,
     xe, ae, ge, mx, ag, wg, xt, g3, w_fwd, w_back,
     ow_f, ow_cols, ow_rows, d1_f, d1_rows, images, sg, sg_flat,
-    dw, pair_out, pair_in, plane_out, plane_in, z_out, z_in, z_all, gathered,
-    plane, high, stat_send, stat_recv, halo_send, halo_recv, sum_send, sum_recv,
+    dw, p1, reach, pair_out, pair_in, plane_out, plane_in, z_out, z_in, z_all, gathered,
+    stats, plane, high, load_sem,
+    stat_send, stat_recv, halo_send, halo_recv, sum_send, sum_recv,
 ):
     me = place()
     frame, row, core, y, z_hi = (me["frame"], me["row"], me["core"], me["y"], me["z_hi"])
     z = z_hi * 4 + me["z_lo"]
     slot = frame * 4 + y
+    clip_slot = row * 4 + frame
+    clip_line = clip_peers(me)
     plane_line, z_line, high_line = (plane_peers(me), z_peers(me), high_peers(me))
     partner = device(me, core=1 - core)
     above, below = (neighbour(me, 0, -1), neighbour(me, 0, 1))
-    corners = [neighbour(me, f, r) for f in (-1, 1) for r in (-1, 1)]
 
     barrier = pltpu.get_barrier_semaphore()
-    greeted = [p for _, p in z_line] + [above, below] + corners
-    greeted += [p for _, p in plane_line] + [partner]
+    greeted = clip_line + [partner] + [
+        device(me, z_hi=(z_hi + dz) % 4, z_lo=(me["z_lo"] + dl) % 4)
+        for dz in range(4)
+        for dl in range(1, 4)
+    ]
     for peer in greeted:
         pl.semaphore_signal(
             barrier, inc=1, device_id=peer, device_id_type=pl.DeviceIdType.MESH
         )
 
-    def plane_start(turn, first, second):
-        plane[turn, slot, 0:1, :] = first
-        plane[turn, slot, 1:2, :] = second
+    own_strip = (pl.ds(2, 4), pl.ds(1, 8))
+    loads = [
+        (x_hbm, xe.at[own_strip]),
+        (score_hbm, sg.at[:, pl.ds(1, 2)]),
+        (w_hbm, w_ref),
+        (ow_hbm, ow_ref),
+        (d1_hbm, d1_ref),
+        (gain1_hbm, gain1_ref),
+        (gain2_hbm, gain2_ref),
+        (d2_hbm, d2_ref),
+        (pick_first_hbm, pick_first),
+        (pick_second_hbm, pick_second),
+        (pick_second_back_hbm, pick_second_back),
+        (pick_first_back_hbm, pick_first_back),
+    ]
+    loads = [
+        pltpu.make_async_copy(src, dst, load_sem.at[index])
+        for index, (src, dst) in enumerate(loads)
+    ]
+    for load in loads:
+        load.start()
+
+    def stats_start(turn, first, second):
+        stats[turn, clip_slot, 0:1, :] = first
+        stats[turn, clip_slot, 1:2, :] = second
+        mine = stats.at[turn, clip_slot]
+        for peer in clip_line:
+            push(mine, mine, peer, stat_send.at[turn], stat_recv.at[turn])
+
+    def stats_wait(turn):
+        others = stats.at[turn, pl.ds(0, 63)]
+        arrived(others, stat_recv.at[turn])
+        arrived(others, stat_send.at[turn])
+
+    def moments_end(turn):
+        stats_wait(turn)
+        parts = stats[turn]
+        sums = jnp.sum(parts, axis=0)
+        mean = group_total(tile(sums[0:1])) / (4.0 * PER_CLIP)
+        apart = parts - mean[0:2]
+        spread = jnp.sum(apart * apart, axis=0)
+        total = group_total(tile(sums[1:2] + float(LOCAL) * spread[0:1]))
+        return (mean[0:1], lax.rsqrt(total[0:1] / (4.0 * LOCAL * PER_CLIP) + EPSILON))
+
+    def sums_end(turn):
+        stats_wait(turn)
+        sums = jnp.sum(stats[turn], axis=0) / (4.0 * LOCAL * PER_CLIP)
+        return (group_total(tile(sums[0:1]))[0:1], group_total(tile(sums[1:2]))[0:1])
+
+    def plane_start(first, second):
+        plane[slot, 0:1, :] = first
+        plane[slot, 1:2, :] = second
         for _, peer in plane_line:
-            push(plane.at[turn, slot], plane.at[turn, slot], peer, stat_send.at[turn, 0], stat_recv.at[turn, 0])
-
-    def plane_wait(turn):
-        others = plane.at[turn, pl.ds(0, 15)]
-        arrived(others, stat_recv.at[turn, 0])
-        arrived(others, stat_send.at[turn, 0])
-
-    def high_start(turn, first, second):
-        high[turn, z_hi, 0:1, :] = first
-        high[turn, z_hi, 1:2, :] = second
+            push(plane.at[slot], plane.at[slot], peer, stat_send.at[3], stat_recv.at[3])
+
+    def plane_to_high():
+        others = plane.at[pl.ds(0, 15)]
+        arrived(others, stat_recv.at[3])
+        arrived(others, stat_send.at[3])
+        high[z_hi] = jnp.sum(plane[...], axis=0)
         for _, peer in high_line:
-            push(high.at[turn, z_hi], high.at[turn, z_hi], peer, stat_send.at[turn, 1], stat_recv.at[turn, 1])
-
-    def high_wait(turn):
-        others = high.at[turn, pl.ds(0, 3)]
-        arrived(others, stat_recv.at[turn, 1])
-        arrived(others, stat_send.at[turn, 1])
-
-    def moments_middle(turn):
-        plane_wait(turn)
-        means, squares = (plane[turn, :, 0, :], plane[turn, :, 1, :])
-        mean = group_total(tile(jnp.sum(means, axis=0, keepdims=True))) / 64.0
-        apart = means - mean[0:1]
-        total = jnp.sum(squares + float(LOCAL) * (apart * apart), axis=0, keepdims=True)
-        high_start(turn, mean[0:1], group_total(tile(total))[0:1])
-
-    def moments_end(turn):
-        high_wait(turn)
-        means, squares = (high[turn, :, 0, :], high[turn, :, 1, :])
-        mean = jnp.sum(means, axis=0, keepdims=True) / 4.0
-        apart = means - mean
-        total = jnp.sum(squares + (64.0 * LOCAL) * (apart * apart), axis=0, keepdims=True)
-        return (mean, lax.rsqrt(total / (4.0 * LOCAL * PER_CLIP) + EPSILON))
-
-    def sums_middle(turn):
-        plane_wait(turn)
-        sums = jnp.sum(plane[turn], axis=0)
-        high_start(turn, group_total(tile(sums[0:1]))[0:1], group_total(tile(sums[1:2]))[0:1])
-
-    def sums_end(turn):
-        high_wait(turn)
-        means = jnp.sum(high[turn], axis=0) / (4.0 * LOCAL * PER_CLIP)
-        return (means[0:1], means[1:2])
+            push(high.at[z_hi], high.at[z_hi], peer, stat_send.at[4], stat_recv.at[4])
+
+    def high_end():
+        others = high.at[pl.ds(0, 3)]
+        arrived(others, stat_recv.at[4])
+        arrived(others, stat_send.at[4])
+        sums = jnp.sum(high[...], axis=0) / (4.0 * LOCAL * PER_CLIP)
+        return (group_total(tile(sums[0:1]))[0:1], group_total(tile(sums[1:2]))[0:1])
 
     def local_moments(read):
         zero = jnp.zeros((1, 128), WIDE)
@@ -223,6 +267,26 @@
             return acc + jnp.sum(apart * apart, axis=0, keepdims=True)
 
         return (mean, lax.fori_loop(0, 4, squares, zero))
+
+    def column_copies(t, values):
+        here = pl.ds(t * 256, 256)
+        values = values.astype(LOW)
+        wide = values.astype(WIDE)
+        column = lax.broadcasted_iota(jnp.int32, wide.shape, 0) % 32
+        g3[here, 128:256] = values
+        g3[here, 0:128] = jnp.where(column == 31, 0.0, pltpu.roll(wide, 255, 0)).astype(LOW)
+        g3[here, 256:384] = jnp.where(column == 0, 0.0, pltpu.roll(wide, 1, 0)).astype(LOW)
+
+    def acts_window(i, j):
+        return jnp.concatenate([xt[j, i + t] for t in range(4)], axis=1)
+
+    def against_acts(result):
+        for i in range(3):
+            for j in range(3):
+                product = wide_dot(acts_window(i, j), g3[...])
+                for c in range(3):
+                    first = ((i * 3 + j) * 3 + c) * 128
+                    result[first : first + 128, :] = product[:, c * 128 : (c + 1) * 128]
 
     def halo_start(turn, src, dst, own_row, own_frames, to_frames, frame_step):
         def go(index, source, target, peer):
@@ -260,28 +324,28 @@
         return (position >= low) & (position < high_end)
 
     def own_input(t):
-        return x_ref[t].astype(WIDE).reshape(256, 128)
-
+        return xe[t + 2, 1:9].astype(WIDE).reshape(256, 128)
+
+    loads[0].wait()
     mean, squares = local_moments(own_input)
-    xe[2:6, 1:9] = x_ref[...]
-    sg[:, 1:3] = score_ref[...]
+    loads[1].wait()
     pl.semaphore_wait(barrier, len(greeted))
-    plane_start(0, mean, squares)
-    halo_start(0, x_ref, xe, 0, (0, 2, 2), 0, 1)
-    push(score_ref.at[:, 1], sg.at[:, 0], below, halo_send.at[0, 5], halo_recv.at[0, 5])
-    push(score_ref.at[:, 0], sg.at[:, 3], above, halo_send.at[0, 6], halo_recv.at[0, 6])
+    stats_start(0, mean, squares)
+    halo_start(0, xe, xe, 1, (2, 4, 2), 0, 1)
+    push(sg.at[:, 2], sg.at[:, 0], below, halo_send.at[0, 5], halo_recv.at[0, 5])
+    push(sg.at[:, 1], sg.at[:, 3], above, halo_send.at[0, 6], halo_recv.at[0, 6])
+    for load in loads[2:]:
+        load.wait()
 
     @pl.loop(0, 9)
     def _(tap):
         for c in range(3):
             w_fwd[pl.ds(tap * 128, 128), c * 128 : (c + 1) * 128] = w_ref[tap * 3 + c]
 
-    moments_middle(0)
-
     ow_f[...] = jnp.zeros((128, 128), WIDE)
-    ow_f[:, 0:3] = ow_ref[...].astype(WIDE)
-    colours = ow_f[...]
-    colours_t = colours.T
+    ow_f[0:3, :] = ow_ref[...].astype(WIDE)
+    colours_t = ow_f[...]
+    colours = colours_t.T
     for c in range(32):
         ow_cols[c * 128 : (c + 1) * 128, :] = (
             colours if c == 0 else pltpu.roll(colours, 3 * c, 1)
@@ -291,8 +355,10 @@
         ).astype(LOW)
     for k in range(4):
         d1_f[...] = jnp.zeros((128, 128), WIDE)
-        for l in range(4):
-            d1_f[3 * l : 3 * l + 3, 0:64] = d1_ref[k * 4 + l].astype(WIDE)
+        for colour in range(3):
+            taps = d1_ref[k * 3 + colour].astype(WIDE)
+            for l in range(4):
+                d1_f[3 * l + colour : 3 * l + colour + 1, 0:64] = taps[l : l + 1]
         single = d1_f[...]
         double = single + pltpu.roll(pltpu.roll(single, 64, 1), 6, 0)
         for p in range(8):
@@ -330,14 +396,21 @@
         mx[t] = (xe[t + 2, 1:9].astype(WIDE).reshape(256, 128) + branch).astype(LOW)
 
     mean, squares = local_moments(lambda t: mx[t].astype(WIDE))
-    plane_start(1, mean, squares)
+    stats_start(1, mean, squares)
 
     @pl.loop(0, 6)
     def _(t):
         for j in range(3):
             xt[j, t] = ae[t, j : j + 8].reshape(256, 128).astype(WIDE).T.astype(LOW)
 
-    moments_middle(1)
+    column = lax.broadcasted_iota(jnp.int32, (1024, 128), 0) % 32
+    tap_lane = lax.broadcasted_iota(jnp.int32, (1024, 128), 1)
+    reached = ((tap_lane != 0) | (column < 31)) & ((tap_lane != 2) | (column > 0))
+    reached = jnp.where(reached, 1.0, 0.0).astype(LOW)
+    for i in range(3):
+        for j in range(3):
+            reach[i * 3 + j] = wide_dot(acts_window(i, j), reached)
+
     mean2, inverse2 = moments_end(1)
 
     def normed_second(t):
@@ -358,6 +431,12 @@
     images[1] = image.astype(LOW)
     push(images.at[1], images.at[0], below, halo_send.at[1, 5], halo_recv.at[1, 5])
     push(images.at[1], images.at[2], above, halo_send.at[1, 6], halo_recv.at[1, 6])
+
+    @pl.loop(0, 4)
+    def _(t):
+        column_copies(t, normed_second(t))
+
+    against_acts(p1)
     sg_flat[...] = sg[...].reshape(64, 128)
     score = jnp.concatenate([sg_flat[pl.ds(p, 8, stride=8), :] for p in range(8)], axis=0)
     for index in (5, 6):
@@ -436,6 +515,7 @@
         here = pl.ds(t * 256, 256)
         weighted = ag[here, :] * silu_slope(normed * gain2) * gain2
         ag[here, :] = weighted
+        column_copies(t, weighted * inverse2)
         return (
             acc[0] + jnp.sum(weighted, axis=0, keepdims=True),
             acc[1] + jnp.sum(weighted * normed, axis=0, keepdims=True),
@@ -443,8 +523,8 @@
 
     zeros = (jnp.zeros((1, 128), WIDE), jnp.zeros((1, 128), WIDE))
     sums = lax.fori_loop(0, 4, weigh, zeros)
-    plane_start(2, *sums)
-    sums_middle(2)
+    stats_start(2, *sums)
+    against_acts(dw)
     first_mean, second_mean = sums_end(2)
 
     @pl.loop(0, 4)
@@ -452,28 +532,60 @@
         here = pl.ds(t * 256, 256)
         grad = (ag[here, :] - first_mean - normed_second(t) * second_mean) * inverse2
         ag[here, :] = grad
-        low = grad.astype(LOW)
-        ge[t, 1:9] = low.reshape(8, 32, 128)
-        grad = low.astype(WIDE)
-        column = lax.broadcasted_iota(jnp.int32, grad.shape, 0) % 32
-        g3[here, 128:256] = low
-        g3[here, 0:128] = jnp.where(column == 31, 0.0, pltpu.roll(grad, 255, 0)).astype(LOW)
-        g3[here, 256:384] = jnp.where(column == 0, 0.0, pltpu.roll(grad, 1, 0)).astype(LOW)
+        ge[t, 1:9] = grad.astype(LOW).reshape(8, 32, 128)
 
     halo_start(1, ge, ge, 1, (0, 0, 0), 4, -1)
 
-    for i in range(3):
-        for j in range(3):
-            acts = jnp.concatenate([xt[j, i + t] for t in range(4)], axis=1)
-            product = wide_dot(acts, g3[...])
-            for c in range(3):
-                first = ((i * 3 + j) * 3 + c) * 128
-                dw[first : first + 128, :] = product[:, c * 128 : (c + 1) * 128]
+    first_part, second_part = (first_mean * inverse2, second_mean * inverse2)
+    for i in range(9):
+        for c in range(3):
+            rows = slice((i * 3 + c) * 128, (i * 3 + c) * 128 + 128)
+            dw[rows, :] = (
+                dw[rows, :] - reach[i, :, c : c + 1] * first_part - p1[rows, :] * second_part
+            )
     dw[3456:3520, :] = jnp.zeros((64, 128), WIDE)
     theirs = pl.ds(pl.multiple_of((1 - core) * 1728, 64), 1792)
     ours = pl.ds(pl.multiple_of(core * 1728, 64), 1792)
-    pair_out[...] = dw[theirs, :].astype(LOW)
-    push(pair_out, pair_in, partner, sum_send.at[0], sum_recv.at[0])
+    chunks = (pl.ds(0, 64), pl.ds(64, 48))
+    pair_out[...] = dw[theirs, :].astype(LOW).reshape(16, 112, 128)
+    for turn, chunk in enumerate(chunks):
+        push(pair_out.at[:, chunk], pair_in.at[:, chunk], partner, sum_send.at[turn], sum_recv.at[turn])
+
+    for turn, chunk in enumerate(chunks):
+        arrived(pair_in.at[:, chunk], sum_recv.at[turn])
+        arrived(pair_in.at[:, chunk], sum_send.at[turn])
+        mine = dw[ours, :].reshape(16, 112, 128)[:, chunk.start : chunk.start + chunk.size]
+        plane_out[:, chunk] = (mine + pair_in[:, chunk].astype(WIDE)).astype(LOW)
+        for other, peer in plane_line:
+            push(
+                plane_out.at[other, chunk],
+                plane_in.at[slot, chunk],
+                peer,
+                sum_send.at[2 + turn],
+                sum_recv.at[2 + turn],
+            )
+        plane_in[slot, chunk] = plane_out[slot, chunk]
+
+    tiles = (range(0, 4), range(4, 7))
+    owns = (me["z_lo"] == 0, (me["z_lo"] == 2) & (z_hi < 3))
+    for turn, chunk in enumerate(chunks):
+        others = plane_in.at[pl.ds(0, 15), chunk]
+        arrived(others, sum_recv.at[2 + turn])
+        arrived(others, sum_send.at[2 + turn])
+        total = jnp.sum(plane_in[:, chunk].astype(WIDE), axis=0).astype(LOW)
+        for index, part in enumerate(tiles[turn]):
+            z_out[part] = total[index * 16 : (index + 1) * 16]
+            owner = (index, 2 * turn)
+
+            @pl.when((z_hi != owner[0]) | (me["z_lo"] != owner[1]))
+            def _():
+                push(
+                    z_out.at[part],
+                    z_in.at[z],
+                    device(me, z_hi=owner[0], z_lo=owner[1]),
+                    sum_send.at[4 + turn],
+                    sum_recv.at[4],
+                )
 
     halo_wait(1, ge, 0, 4)
 
@@ -504,68 +616,89 @@
         )
 
     sums = lax.fori_loop(0, 4, back_step, zeros)
-    plane_start(3, *sums)
-
-    arrived(pair_in, sum_recv.at[0])
-    arrived(pair_in, sum_send.at[0])
-    plane_out[...] = (dw[ours, :] + pair_in[...].astype(WIDE)).astype(LOW).reshape(16, 112, 128)
-    for other, peer in plane_line:
-        push(plane_out.at[other], plane_in.at[slot], peer, sum_send.at[1], sum_recv.at[1])
-    plane_in[slot] = plane_out[slot]
-
-    sums_middle(3)
-
-    arrived(plane_in.at[pl.ds(0, 15)], sum_recv.at[1])
-    arrived(plane_in.at[pl.ds(0, 15)], sum_send.at[1])
-    z_out[0:14] = jnp.sum(plane_in[...].astype(WIDE), axis=0).reshape(14, 8, 128)
-    z_out[14:16] = jnp.zeros((2, 8, 128), WIDE)
-    for other, peer in z_line:
-        push(z_out.at[other], z_in.at[z], peer, sum_send.at[2], sum_recv.at[2])
-    z_in[z] = z_out[z]
-
-    first_mean, second_mean = sums_end(3)
+    plane_start(*sums)
+
+    for turn in range(2):
+
+        @pl.when(owns[turn])
+        def _():
+            part = z_hi + 4 * turn
+            z_in[z] = z_out[part]
+            arrived(z_in.at[pl.ds(0, 15)], sum_recv.at[4])
+            z_all[part] = jnp.sum(z_in[...].astype(WIDE), axis=0).astype(LOW)
+            for _, peer in z_line:
+                push(z_all.at[part], z_all.at[part], peer, sum_send.at[6], sum_recv.at[6 + turn])
+
+    plane_to_high()
+
+    half, other_half = (gathered.at[core], gathered.at[1 - core])
+    for turn, chunk in enumerate(chunks):
+        count = len(tiles[turn])
+
+        @pl.when(owns[turn])
+        def _():
+            arrived(z_all.at[pl.ds(0, count - 1)], sum_recv.at[6 + turn])
+            arrived(z_out.at[pl.ds(0, count - 1)], sum_send.at[4 + turn])
+            arrived(z_in.at[pl.ds(0, 15)], sum_send.at[6])
+
+        @pl.when(jnp.logical_not(owns[turn]))
+        def _():
+            arrived(z_all.at[pl.ds(0, count)], sum_recv.at[6 + turn])
+            arrived(z_out.at[pl.ds(0, count)], sum_send.at[4 + turn])
+
+        first = tiles[turn].start
+        half[slot, chunk] = z_all[first : first + count].reshape(count * 16, 128)
+        for _, peer in plane_line:
+            push(
+                half.at[slot, chunk],
+                half.at[slot, chunk],
+                peer,
+                sum_send.at[8 + turn],
+                sum_recv.at[8 + turn],
+            )
+
+    first_mean, second_mean = high_end()
 
     @pl.loop(0, 4)
     def _(t):
         grad = (wg[t] - first_mean - normed_first(t) * second_mean) * inverse1
         out_ref[t] = (ag[pl.ds(t * 256, 256), :] + grad).astype(LOW).reshape(8, 32, 128)
 
-    arrived(z_in.at[pl.ds(0, 15)], sum_recv.at[2])
-    arrived(z_in.at[pl.ds(0, 15)], sum_send.at[2])
-    z_all[z] = jnp.sum(z_in[...], axis=0)
-    for _, peer in z_line:
-        push(z_all.at[z], z_all.at[z], peer, sum_send.at[3], sum_recv.at[3])
-    arrived(z_all.at[pl.ds(0, 15)], sum_recv.at[3])
-    arrived(z_all.at[pl.ds(0, 15)], sum_send.at[3])
-    half = gathered.at[core]
-    half[slot] = z_all[0:14].reshape(112, 128).astype(LOW)
-    for _, peer in plane_line:
-        push(half.at[slot], half.at[slot], peer, sum_send.at[4], sum_recv.at[4])
-    arrived(half.at[pl.ds(0, 15)], sum_recv.at[4])
-    arrived(half.at[pl.ds(0, 15)], sum_send.at[4])
-    push(half, half, partner, sum_send.at[5], sum_recv.at[5])
-    arrived(half, sum_recv.at[5])
-    arrived(half, sum_send.at[5])
-
-    def square(part, acc):
-        for core_part in range(2):
-            piece = gathered[core_part, part].astype(WIDE)
-            piece = jnp.where(
-                lax.broadcasted_iota(jnp.int32, piece.shape, 0) + part * 112 < 1728, piece, 0.0
-            )
-            acc = acc + jnp.sum((piece * piece).reshape(14, 8, 128), axis=0)
-        return acc
-
-    total = lax.fori_loop(0, 16, square, jnp.zeros((8, 128), WIDE))
-    scale = lax.rsqrt(jnp.sum(total, keepdims=True) / (3456.0 * 128.0) + EPSILON)
-
-    @pl.loop(0, 15)
-    def _(part):
-        for core_part in range(2):
-            upd_ref[core_part, pl.ds(part * 112, 112), :] = gathered[core_part, part].astype(WIDE) * scale
-
-    for core_part in range(2):
-        upd_ref[core_part, 1680:1728, :] = gathered[core_part, 15, 0:48].astype(WIDE) * scale
+    def squares_of(part_of, chunk):
+        def add(part, acc):
+            piece = part_of[part, chunk].astype(WIDE)
+            return acc + jnp.sum((piece * piece).reshape(chunk.size // 8, 8, 128), axis=0)
+
+        total = lax.fori_loop(0, 15, add, jnp.zeros((8, 128), WIDE))
+        if chunk.start == 0:
+            piece = part_of[15, 0:48].astype(WIDE)
+            total = total + jnp.sum((piece * piece).reshape(6, 8, 128), axis=0)
+        return total
+
+    squares = []
+    for turn, chunk in enumerate(chunks):
+        others = half.at[pl.ds(0, 15), chunk]
+        arrived(others, sum_recv.at[8 + turn])
+        arrived(others, sum_send.at[8 + turn])
+        push(half.at[:, chunk], half.at[:, chunk], partner, sum_send.at[10 + turn], sum_recv.at[10 + turn])
+        squares.append(squares_of(half, chunk))
+    for turn, chunk in enumerate(chunks):
+        arrived(other_half.at[:, chunk], sum_recv.at[10 + turn])
+        arrived(half.at[:, chunk], sum_send.at[10 + turn])
+        squares.append(squares_of(other_half, chunk))
+    total = (squares[0] + squares[1]) + (squares[2] + squares[3])
+    mean = jnp.sum(total, keepdims=True) / (3456.0 * 128.0)
+    scale_ref[...] = jnp.broadcast_to(lax.rsqrt(mean + EPSILON), (8, 128))
+    summed_ref[...] = gathered[...]
+
+
+def finish_kernel(grad_ref, summed_ref, scale_ref, out_ref, upd_ref):
+    out_ref[...] = grad_ref[...]
+    scale = scale_ref[0:1, :]
+    for core in range(2):
+        values = summed_ref[core, 0:15].reshape(1680, 128)
+        upd_ref[core, 0:1680, :] = values.astype(WIDE) * scale
+        upd_ref[core, 1680:1728, :] = summed_ref[core, 15, 0:48].astype(WIDE) * scale
 
 
 def shards(
@@ -576,39 +709,53 @@
     wide = lambda *shape: pltpu.VMEM(shape, WIDE)
     dma = pltpu.SemaphoreType.DMA
     picks = selections()
-    input_grad, update = pl.pallas_call(
+    hbm = pl.BlockSpec(memory_space=pltpu.HBM)
+    input_grad, summed, scale = pl.pallas_call(
         step_kernel,
         out_shape=(
             jax.ShapeDtypeStruct((4, 8, 32, 128), LOW),
-            jax.ShapeDtypeStruct((2, 1728, 128), WIDE),
+            jax.ShapeDtypeStruct((2, 16, 112, 128), LOW),
+            jax.ShapeDtypeStruct((8, 128), WIDE),
         ),
-        in_specs=[vmem] * 12,
-        out_specs=(vmem, vmem),
+        in_specs=[hbm] * 12,
+        out_specs=(vmem, vmem, vmem),
         scratch_shapes=[
+            wide(1, 128), low(27, 128, 128), wide(1, 128), low(3, 128), low(12, 4, 64),
+            low(32, 64, 128), low(160, 96), low(64, 40), wide(24, 64), wide(32, 96),
             low(6, 10, 32, 128), low(6, 10, 32, 128), low(6, 10, 32, 128),
             low(4, 256, 128), wide(1024, 128), wide(4, 256, 128),
             low(3, 6, 128, 256), low(1024, 384), low(1152, 384), low(1152, 384),
             wide(128, 128), low(4096, 128), low(128, 4096), wide(128, 128), low(512, 1024),
             low(3, 32, 128), wide(2, 4, 8, 128), wide(64, 128),
-            wide(3520, 128), low(1792, 128), low(1792, 128), low(16, 112, 128), low(16, 112, 128),
-            wide(16, 8, 128), wide(16, 8, 128), wide(16, 8, 128), low(2, 16, 112, 128),
-            wide(4, 16, 2, 128), wide(4, 4, 2, 128),
-            dma((4, 2)), dma((4, 2)), dma((2, 7)), dma((2, 7)), dma((6,)), dma((6,)),
+            wide(3520, 128), wide(3456, 128), wide(9, 128, 128), low(16, 112, 128), low(16, 112, 128), low(16, 112, 128), low(16, 112, 128),
+            low(7, 16, 128), low(16, 16, 128), low(7, 16, 128), low(2, 16, 112, 128),
+            wide(3, 64, 2, 128), wide(16, 2, 128), wide(4, 2, 128),
+            dma((12,)), dma((5,)), dma((5,)), dma((2, 7)), dma((2, 7)), dma((12,)), dma((12,)),
         ],
         compiler_params=pltpu.CompilerParams(
-            collective_id=1, has_side_effects=True, vmem_limit_bytes=48 * 1024 * 1024
+            collective_id=1, has_side_effects=True, vmem_limit_bytes=64 * 1024 * 1024
         ),
     )(
         block_input[0],
         gain_first.reshape(1, 128),
         conv_weight.reshape(27, 128, 128),
         gain_second.reshape(1, 128),
-        out_weight,
-        disc_first.reshape(16, 3, 64),
+        out_weight.T,
+        disc_first[0].transpose(0, 2, 1, 3).reshape(12, 4, 64),
         disc_second.reshape(32, 64, 128),
         score_grad[0],
         *picks,
     )
+    input_grad, update = pl.pallas_call(
+        finish_kernel,
+        out_shape=(
+            jax.ShapeDtypeStruct((4, 8, 32, 128), LOW),
+            jax.ShapeDtypeStruct((2, 1728, 128), WIDE),
+        ),
+        in_specs=[vmem] * 3,
+        out_specs=(vmem, vmem),
+        compiler_params=pltpu.CompilerParams(vmem_limit_bytes=64 * 1024 * 1024),
+    )(input_grad, summed, scale)
     return (input_grad[None], update.reshape(conv_weight.shape))
 
 

time: 121 us -> 101 us (0.83)
  local copies, waits for them, and re-layouts: 11.5 us -> 0 us
  Pallas kernels: 109 us -> 100 us
    unnamed x24 -> x0, local copies, waits for them, and re-layouts: 11.5 us -> none
    pallas_call x1, Pallas kernels: 109 us -> 97.5 us  [shards(): pl.pallas_call(step_kernel, out_shape=(jax.ShapeDtypeStruct((4, 8, 32, 12...]
    pallas_call x0 -> x1, Pallas kernels: none -> 2.57 us  [shards(): pl.pallas_call(finish_kernel, out_shape=(jax.ShapeDtypeStruct((4, 8, 32,...]
where the time goes in v3:
time: 101 us
  Pallas kernels  100 us (99%)
    pallas_call x1, Pallas kernels, shards(): pl.pallas_call(step_kernel, out_shape=(jax.ShapeDtypeStruct((4, 8, 32, 12...  97.5 us
    pallas_call x1, Pallas kernels, shards(): pl.pallas_call(finish_kernel, out_shape=(jax.ShapeDtypeStruct((4, 8, 32,...  2.57 us

profile of v3, /device:TPU:1, one launch (start us, length us, event | category | flops | bytes accessed | tf_op | source)
XLA Modules:
  0.0 100.7 jit_solution(570503348848899191)
XLA Ops:
  0.6 97.5 %shard_map.131 = (bf16[4,8,32,128]{3,2,1,0:T(8,128)(2,1)}, bf16[2,16,112,128]{3,2,1,0:T(8,128)(2,1)}, f32[8,128]{1,0:T(8,128)}) custom-call(bf16[4,8,32,128]{3,2,1,0:T(8,128)(2,1)} %bitcast.16, f32[1,128]{1,0:T(1,128)} %bitcast.20, bf16[27,128,128]{2,1,0:T(8,128)(2,1)} %bitcast.14, f32[1,128]{1,0:T(1,128)} %bitcast.21, bf16[3,128]{1,0:T(4,128)(2,1)} %bitcast.19, ...), custom_call_target="tpu_custom_call" | custom-call | tf_op jit(solution)/shard_map/pallas_call | solution.py:713
  98.1 2.6 %shard_map.132 = (bf16[4,8,32,128]{3,2,1,0:T(8,128)(2,1)}, f32[2,1728,128]{2,1,0:T(8,128)}) custom-call(bf16[4,8,32,128]{3,2,1,0:T(8,128)(2,1)} %get-tuple-element.7.grad_ref, bf16[2,16,112,128]{3,2,1,0:T(8,128)(2,1)} %get-tuple-element.8.summed_ref, f32[8,128]{1,0:T(8,128)} %get-tuple-element.9.scale_ref), custom_call_target="tpu_custom_call" | custom-call | tf_op jit(solution)/shard_map/pallas_call | solution.py:749

commit v4 on v3

--- a/solution.py
+++ b/solution.py
@@ -155,8 +155,8 @@
 def step_kernel(
     x_hbm, gain1_hbm, w_hbm, gain2_hbm, ow_hbm, d1_hbm, d2_hbm, score_hbm,
     pick_first_hbm, pick_second_hbm, pick_second_back_hbm, pick_first_back_hbm,
-    out_ref, summed_ref, scale_ref,
-    gain1_ref, w_ref, gain2_ref, ow_ref, d1_ref, d2_ref,
+    grad_hbm, summed_hbm, scale_ref,
+    out_ref, gain1_ref, w_ref, gain2_ref, ow_ref, d1_ref, d2_ref,
     pick_first, pick_second, pick_second_back, pick_first_back,
     xe, ae, ge, mx, ag, wg, xt, g3, w_fwd, w_back,
     ow_f, ow_cols, ow_rows, d1_f, d1_rows, images, sg, sg_flat,
@@ -207,11 +207,13 @@
     for load in loads:
         load.start()
 
-    def stats_start(turn, first, second):
+    def stats_start(turn, first, second, before_nearest=lambda: None):
         stats[turn, clip_slot, 0:1, :] = first
         stats[turn, clip_slot, 1:2, :] = second
         mine = stats.at[turn, clip_slot]
-        for peer in clip_line:
+        for index, peer in enumerate(clip_line):
+            if index == 48:
+                before_nearest()
             push(mine, mine, peer, stat_send.at[turn], stat_recv.at[turn])
 
     def stats_wait(turn):
@@ -330,8 +332,7 @@
     mean, squares = local_moments(own_input)
     loads[1].wait()
     pl.semaphore_wait(barrier, len(greeted))
-    stats_start(0, mean, squares)
-    halo_start(0, xe, xe, 1, (2, 4, 2), 0, 1)
+    stats_start(0, mean, squares, lambda: halo_start(0, xe, xe, 1, (2, 4, 2), 0, 1))
     push(sg.at[:, 2], sg.at[:, 0], below, halo_send.at[0, 5], halo_recv.at[0, 5])
     push(sg.at[:, 1], sg.at[:, 3], above, halo_send.at[0, 6], halo_recv.at[0, 6])
     for load in loads[2:]:
@@ -567,7 +568,8 @@
         plane_in[slot, chunk] = plane_out[slot, chunk]
 
     tiles = (range(0, 4), range(4, 7))
-    owns = (me["z_lo"] == 0, (me["z_lo"] == 2) & (z_hi < 3))
+    own_tile = z % 8
+    owns = (own_tile < 4, (own_tile >= 4) & (own_tile < 7))
     for turn, chunk in enumerate(chunks):
         others = plane_in.at[pl.ds(0, 15), chunk]
         arrived(others, sum_recv.at[2 + turn])
@@ -575,17 +577,17 @@
         total = jnp.sum(plane_in[:, chunk].astype(WIDE), axis=0).astype(LOW)
         for index, part in enumerate(tiles[turn]):
             z_out[part] = total[index * 16 : (index + 1) * 16]
-            owner = (index, 2 * turn)
-
-            @pl.when((z_hi != owner[0]) | (me["z_lo"] != owner[1]))
-            def _():
-                push(
-                    z_out.at[part],
-                    z_in.at[z],
-                    device(me, z_hi=owner[0], z_lo=owner[1]),
-                    sum_send.at[4 + turn],
-                    sum_recv.at[4],
-                )
+            for owner in (part, part + 8):
+
+                @pl.when(z != owner)
+                def _():
+                    push(
+                        z_out.at[part],
+                        z_in.at[z],
+                        device(me, z_hi=owner // 4, z_lo=owner % 4),
+                        sum_send.at[4 + turn],
+                        sum_recv.at[4],
+                    )
 
     halo_wait(1, ge, 0, 4)
 
@@ -622,12 +624,14 @@
 
         @pl.when(owns[turn])
         def _():
-            part = z_hi + 4 * turn
-            z_in[z] = z_out[part]
+            z_in[z] = z_out[own_tile]
             arrived(z_in.at[pl.ds(0, 15)], sum_recv.at[4])
-            z_all[part] = jnp.sum(z_in[...].astype(WIDE), axis=0).astype(LOW)
-            for _, peer in z_line:
-                push(z_all.at[part], z_all.at[part], peer, sum_send.at[6], sum_recv.at[6 + turn])
+            z_all[own_tile] = jnp.sum(z_in[...].astype(WIDE), axis=0).astype(LOW)
+            mine = z_all.at[own_tile]
+            for step in (-4, 3, -3, 2, -2, 1, -1):
+                other = (z + step) % 16
+                peer = device(me, z_hi=other // 4, z_lo=other % 4)
+                push(mine, mine, peer, sum_send.at[6], sum_recv.at[6 + turn])
 
     plane_to_high()
 
@@ -638,13 +642,13 @@
         @pl.when(owns[turn])
         def _():
             arrived(z_all.at[pl.ds(0, count - 1)], sum_recv.at[6 + turn])
-            arrived(z_out.at[pl.ds(0, count - 1)], sum_send.at[4 + turn])
-            arrived(z_in.at[pl.ds(0, 15)], sum_send.at[6])
+            arrived(z_in.at[pl.ds(0, 2 * count - 1)], sum_send.at[4 + turn])
+            arrived(z_in.at[pl.ds(0, 7)], sum_send.at[6])
 
         @pl.when(jnp.logical_not(owns[turn]))
         def _():
             arrived(z_all.at[pl.ds(0, count)], sum_recv.at[6 + turn])
-            arrived(z_out.at[pl.ds(0, count)], sum_send.at[4 + turn])
+            arrived(z_in.at[pl.ds(0, 2 * count)], sum_send.at[4 + turn])
 
         first = tiles[turn].start
         half[slot, chunk] = z_all[first : first + count].reshape(count * 16, 128)
@@ -664,6 +668,9 @@
         grad = (wg[t] - first_mean - normed_first(t) * second_mean) * inverse1
         out_ref[t] = (ag[pl.ds(t * 256, 256), :] + grad).astype(LOW).reshape(8, 32, 128)
 
+    out_copy = pltpu.make_async_copy(out_ref, grad_hbm, load_sem.at[12])
+    out_copy.start()
+
     def squares_of(part_of, chunk):
         def add(part, acc):
             piece = part_of[part, chunk].astype(WIDE)
@@ -682,23 +689,28 @@
         arrived(others, sum_send.at[8 + turn])
         push(half.at[:, chunk], half.at[:, chunk], partner, sum_send.at[10 + turn], sum_recv.at[10 + turn])
         squares.append(squares_of(half, chunk))
+    own_copy = pltpu.make_async_copy(half, summed_hbm.at[core], load_sem.at[13])
+    own_copy.start()
     for turn, chunk in enumerate(chunks):
         arrived(other_half.at[:, chunk], sum_recv.at[10 + turn])
         arrived(half.at[:, chunk], sum_send.at[10 + turn])
+    other_copy = pltpu.make_async_copy(other_half, summed_hbm.at[1 - core], load_sem.at[14])
+    other_copy.start()
+    for chunk in chunks:
         squares.append(squares_of(other_half, chunk))
     total = (squares[0] + squares[1]) + (squares[2] + squares[3])
     mean = jnp.sum(total, keepdims=True) / (3456.0 * 128.0)
     scale_ref[...] = jnp.broadcast_to(lax.rsqrt(mean + EPSILON), (8, 128))
-    summed_ref[...] = gathered[...]
+    for copy in (out_copy, own_copy, other_copy):
+        copy.wait()
 
 
 def finish_kernel(grad_ref, summed_ref, scale_ref, out_ref, upd_ref):
     out_ref[...] = grad_ref[...]
     scale = scale_ref[0:1, :]
-    for core in range(2):
-        values = summed_ref[core, 0:15].reshape(1680, 128)
-        upd_ref[core, 0:1680, :] = values.astype(WIDE) * scale
-        upd_ref[core, 1680:1728, :] = summed_ref[core, 15, 0:48].astype(WIDE) * scale
+    values = summed_ref[0, 0:15].reshape(1680, 128)
+    upd_ref[0, 0:1680, :] = values.astype(WIDE) * scale
+    upd_ref[0, 1680:1728, :] = summed_ref[0, 15, 0:48].astype(WIDE) * scale
 
 
 def shards(
@@ -718,9 +730,9 @@
             jax.ShapeDtypeStruct((8, 128), WIDE),
         ),
         in_specs=[hbm] * 12,
-        out_specs=(vmem, vmem, vmem),
+        out_specs=(hbm, hbm, vmem),
         scratch_shapes=[
-            wide(1, 128), low(27, 128, 128), wide(1, 128), low(3, 128), low(12, 4, 64),
+            low(4, 8, 32, 128), wide(1, 128), low(27, 128, 128), wide(1, 128), low(3, 128), low(12, 4, 64),
             low(32, 64, 128), low(160, 96), low(64, 40), wide(24, 64), wide(32, 96),
             low(6, 10, 32, 128), low(6, 10, 32, 128), low(6, 10, 32, 128),
             low(4, 256, 128), wide(1024, 128), wide(4, 256, 128),
@@ -730,7 +742,7 @@
             wide(3520, 128), wide(3456, 128), wide(9, 128, 128), low(16, 112, 128), low(16, 112, 128), low(16, 112, 128), low(16, 112, 128),
             low(7, 16, 128), low(16, 16, 128), low(7, 16, 128), low(2, 16, 112, 128),
             wide(3, 64, 2, 128), wide(16, 2, 128), wide(4, 2, 128),
-            dma((12,)), dma((5,)), dma((5,)), dma((2, 7)), dma((2, 7)), dma((12,)), dma((12,)),
+            dma((15,)), dma((5,)), dma((5,)), dma((2, 7)), dma((2, 7)), dma((12,)), dma((12,)),
         ],
         compiler_params=pltpu.CompilerParams(
             collective_id=1, has_side_effects=True, vmem_limit_bytes=64 * 1024 * 1024
@@ -752,8 +764,16 @@
             jax.ShapeDtypeStruct((4, 8, 32, 128), LOW),
             jax.ShapeDtypeStruct((2, 1728, 128), WIDE),
         ),
-        in_specs=[vmem] * 3,
-        out_specs=(vmem, vmem),
+        grid=(2,),
+        in_specs=[
+            pl.BlockSpec((2, 8, 32, 128), lambda half: (half, 0, 0, 0)),
+            pl.BlockSpec((1, 16, 112, 128), lambda half: (half, 0, 0, 0)),
+            pl.BlockSpec((8, 128), lambda half: (0, 0)),
+        ],
+        out_specs=(
+            pl.BlockSpec((2, 8, 32, 128), lambda half: (half, 0, 0, 0)),
+            pl.BlockSpec((1, 1728, 128), lambda half: (half, 0, 0)),
+        ),
         compiler_params=pltpu.CompilerParams(vmem_limit_bytes=64 * 1024 * 1024),
     )(input_grad, summed, scale)
     return (input_grad[None], update.reshape(conv_weight.shape))

time: 101 us -> 99.5 us (0.985)
  Pallas kernels: 100 us -> 98.7 us
    pallas_call x1, Pallas kernels: 97.5 us -> 96.3 us  [shards(): pl.pallas_call(step_kernel, out_shape=(jax.ShapeDtypeStruct((4, 8, 32, 12...]
where the time goes in v4:
time: 99.5 us; the launch traced here: 99.4 us
  Pallas kernels  98.7 us (99%)
    pallas_call x1, Pallas kernels, shards(): pl.pallas_call(step_kernel, out_shape=(jax.ShapeDtypeStruct((4, 8, 32, 12...  96.3 us
    pallas_call x1, Pallas kernels, shards(): pl.pallas_call(finish_kernel, out_shape=(jax.ShapeDtypeStruct((4, 8, 32,...  2.43 us

profile of v4, /device:TPU:1, one launch (start us, length us, event | category | flops | bytes accessed | tf_op | source)
XLA Modules:
  0.0 99.4 jit_solution(15419670735441961290)
XLA Ops:
  0.6 96.3 %shard_map.131 = (bf16[4,8,32,128]{3,2,1,0:T(8,128)(2,1)}, bf16[2,16,112,128]{3,2,1,0:T(8,128)(2,1)}, f32[8,128]{1,0:T(8,128)}) custom-call(bf16[4,8,32,128]{3,2,1,0:T(8,128)(2,1)} %bitcast.16, f32[1,128]{1,0:T(1,128)} %bitcast.20, bf16[27,128,128]{2,1,0:T(8,128)(2,1)} %bitcast.14, f32[1,128]{1,0:T(1,128)} %bitcast.21, bf16[3,128]{1,0:T(4,128)(2,1)} %bitcast.19, ...), custom_call_target="tpu_custom_call" | custom-call | tf_op jit(solution)/shard_map/pallas_call | solution.py:725
  96.9 2.4 %shard_map.132 = (bf16[4,8,32,128]{3,2,1,0:T(8,128)(2,1)}, f32[2,1728,128]{2,1,0:T(8,128)}) custom-call(bf16[4,8,32,128]{3,2,1,0:T(8,128)(2,1)} %get-tuple-element.7.grad_ref, bf16[2,16,112,128]{3,2,1,0:T(8,128)(2,1)} %get-tuple-element.8.summed_ref, f32[8,128]{1,0:T(8,128)} %get-tuple-element.9.scale_ref), custom_call_target="tpu_custom_call" | custom-call | tf_op jit(solution)/shard_map/pallas_call | solution.py:761

commit v5 on v4

--- a/solution.py
+++ b/solution.py
@@ -160,7 +160,7 @@
     pick_first, pick_second, pick_second_back, pick_first_back,
     xe, ae, ge, mx, ag, wg, xt, g3, w_fwd, w_back,
     ow_f, ow_cols, ow_rows, d1_f, d1_rows, images, sg, sg_flat,
-    dw, p1, reach, pair_out, pair_in, plane_out, plane_in, z_out, z_in, z_all, gathered,
+    dw, p1, reach, sums_wide, pair_out, pair_in, plane_out, plane_in, z_out, z_in, z_all, gathered,
     stats, plane, high, load_sem,
     stat_send, stat_recv, halo_send, halo_recv, sum_send, sum_recv,
 ):
@@ -219,7 +219,6 @@
     def stats_wait(turn):
         others = stats.at[turn, pl.ds(0, 63)]
         arrived(others, stat_recv.at[turn])
-        arrived(others, stat_send.at[turn])
 
     def moments_end(turn):
         stats_wait(turn)
@@ -245,7 +244,6 @@
     def plane_to_high():
         others = plane.at[pl.ds(0, 15)]
         arrived(others, stat_recv.at[3])
-        arrived(others, stat_send.at[3])
         high[z_hi] = jnp.sum(plane[...], axis=0)
         for _, peer in high_line:
             push(high.at[z_hi], high.at[z_hi], peer, stat_send.at[4], stat_recv.at[4])
@@ -253,7 +251,6 @@
     def high_end():
         others = high.at[pl.ds(0, 3)]
         arrived(others, stat_recv.at[4])
-        arrived(others, stat_send.at[4])
         sums = jnp.sum(high[...], axis=0) / (4.0 * LOCAL * PER_CLIP)
         return (group_total(tile(sums[0:1]))[0:1], group_total(tile(sums[1:2]))[0:1])
 
@@ -526,7 +523,25 @@
     sums = lax.fori_loop(0, 4, weigh, zeros)
     stats_start(2, *sums)
     against_acts(dw)
+    for i in range(9):
+        for c in range(3):
+            first = (i * 3 + c) * 128
+            sums_wide[first : first + 128, :] = jnp.broadcast_to(reach[i, :, c : c + 1], (128, 128))
+    for array in (dw, p1, sums_wide):
+        array[3456:3520, :] = jnp.zeros((64, 128), WIDE)
     first_mean, second_mean = sums_end(2)
+
+    first_part, second_part = (first_mean * inverse2, second_mean * inverse2)
+    theirs = pl.ds(pl.multiple_of((1 - core) * 1728, 64), 1792)
+    ours = pl.ds(pl.multiple_of(core * 1728, 64), 1792)
+    chunks = (pl.ds(0, 64), pl.ds(64, 48))
+
+    def corrected(rows):
+        return dw[rows, :] - sums_wide[rows, :] * first_part - p1[rows, :] * second_part
+
+    pair_out[...] = corrected(theirs).astype(LOW).reshape(16, 112, 128)
+    for turn, chunk in enumerate(chunks):
+        push(pair_out.at[:, chunk], pair_in.at[:, chunk], partner, sum_send.at[turn], sum_recv.at[turn])
 
     @pl.loop(0, 4)
     def _(t):
@@ -537,24 +552,9 @@
 
     halo_start(1, ge, ge, 1, (0, 0, 0), 4, -1)
 
-    first_part, second_part = (first_mean * inverse2, second_mean * inverse2)
-    for i in range(9):
-        for c in range(3):
-            rows = slice((i * 3 + c) * 128, (i * 3 + c) * 128 + 128)
-            dw[rows, :] = (
-                dw[rows, :] - reach[i, :, c : c + 1] * first_part - p1[rows, :] * second_part
-            )
-    dw[3456:3520, :] = jnp.zeros((64, 128), WIDE)
-    theirs = pl.ds(pl.multiple_of((1 - core) * 1728, 64), 1792)
-    ours = pl.ds(pl.multiple_of(core * 1728, 64), 1792)
-    chunks = (pl.ds(0, 64), pl.ds(64, 48))
-    pair_out[...] = dw[theirs, :].astype(LOW).reshape(16, 112, 128)
-    for turn, chunk in enumerate(chunks):
-        push(pair_out.at[:, chunk], pair_in.at[:, chunk], partner, sum_send.at[turn], sum_recv.at[turn])
-
+    dw[ours, :] = corrected(ours)
     for turn, chunk in enumerate(chunks):
         arrived(pair_in.at[:, chunk], sum_recv.at[turn])
-        arrived(pair_in.at[:, chunk], sum_send.at[turn])
         mine = dw[ours, :].reshape(16, 112, 128)[:, chunk.start : chunk.start + chunk.size]
         plane_out[:, chunk] = (mine + pair_in[:, chunk].astype(WIDE)).astype(LOW)
         for other, peer in plane_line:
@@ -573,7 +573,6 @@
     for turn, chunk in enumerate(chunks):
         others = plane_in.at[pl.ds(0, 15), chunk]
         arrived(others, sum_recv.at[2 + turn])
-        arrived(others, sum_send.at[2 + turn])
         total = jnp.sum(plane_in[:, chunk].astype(WIDE), axis=0).astype(LOW)
         for index, part in enumerate(tiles[turn]):
             z_out[part] = total[index * 16 : (index + 1) * 16]
@@ -642,13 +641,10 @@
         @pl.when(owns[turn])
         def _():
             arrived(z_all.at[pl.ds(0, count - 1)], sum_recv.at[6 + turn])
-            arrived(z_in.at[pl.ds(0, 2 * count - 1)], sum_send.at[4 + turn])
-            arrived(z_in.at[pl.ds(0, 7)], sum_send.at[6])
 
         @pl.when(jnp.logical_not(owns[turn]))
         def _():
             arrived(z_all.at[pl.ds(0, count)], sum_recv.at[6 + turn])
-            arrived(z_in.at[pl.ds(0, 2 * count)], sum_send.at[4 + turn])
 
         first = tiles[turn].start
         half[slot, chunk] = z_all[first : first + count].reshape(count * 16, 128)
@@ -686,14 +682,12 @@
     for turn, chunk in enumerate(chunks):
         others = half.at[pl.ds(0, 15), chunk]
         arrived(others, sum_recv.at[8 + turn])
-        arrived(others, sum_send.at[8 + turn])
         push(half.at[:, chunk], half.at[:, chunk], partner, sum_send.at[10 + turn], sum_recv.at[10 + turn])
         squares.append(squares_of(half, chunk))
     own_copy = pltpu.make_async_copy(half, summed_hbm.at[core], load_sem.at[13])
     own_copy.start()
     for turn, chunk in enumerate(chunks):
         arrived(other_half.at[:, chunk], sum_recv.at[10 + turn])
-        arrived(half.at[:, chunk], sum_send.at[10 + turn])
     other_copy = pltpu.make_async_copy(other_half, summed_hbm.at[1 - core], load_sem.at[14])
     other_copy.start()
     for chunk in chunks:
@@ -701,6 +695,27 @@
     total = (squares[0] + squares[1]) + (squares[2] + squares[3])
     mean = jnp.sum(total, keepdims=True) / (3456.0 * 128.0)
     scale_ref[...] = jnp.broadcast_to(lax.rsqrt(mean + EPSILON), (8, 128))
+
+    for turn in range(3):
+        arrived(stats.at[turn, pl.ds(0, 63)], stat_send.at[turn])
+    arrived(plane.at[pl.ds(0, 15)], stat_send.at[3])
+    arrived(high.at[pl.ds(0, 3)], stat_send.at[4])
+    for turn, chunk in enumerate(chunks):
+        count = len(tiles[turn])
+        arrived(pair_in.at[:, chunk], sum_send.at[turn])
+        arrived(plane_in.at[pl.ds(0, 15), chunk], sum_send.at[2 + turn])
+        arrived(half.at[pl.ds(0, 15), chunk], sum_send.at[8 + turn])
+        arrived(half.at[:, chunk], sum_send.at[10 + turn])
+
+        @pl.when(owns[turn])
+        def _():
+            arrived(z_in.at[pl.ds(0, 2 * count - 1)], sum_send.at[4 + turn])
+            arrived(z_in.at[pl.ds(0, 7)], sum_send.at[6])
+
+        @pl.when(jnp.logical_not(owns[turn]))
+        def _():
+            arrived(z_in.at[pl.ds(0, 2 * count)], sum_send.at[4 + turn])
+
     for copy in (out_copy, own_copy, other_copy):
         copy.wait()
 
@@ -739,7 +754,7 @@
             low(3, 6, 128, 256), low(1024, 384), low(1152, 384), low(1152, 384),
             wide(128, 128), low(4096, 128), low(128, 4096), wide(128, 128), low(512, 1024),
             low(3, 32, 128), wide(2, 4, 8, 128), wide(64, 128),
-            wide(3520, 128), wide(3456, 128), wide(9, 128, 128), low(16, 112, 128), low(16, 112, 128), low(16, 112, 128), low(16, 112, 128),
+            wide(3520, 128), wide(3520, 128), wide(9, 128, 128), wide(3520, 128), low(16, 112, 128), low(16, 112, 128), low(16, 112, 128), low(16, 112, 128),
             low(7, 16, 128), low(16, 16, 128), low(7, 16, 128), low(2, 16, 112, 128),
             wide(3, 64, 2, 128), wide(16, 2, 128), wide(4, 2, 128),
             dma((15,)), dma((5,)), dma((5,)), dma((2, 7)), dma((2, 7)), dma((12,)), dma((12,)),

time: 99.5 us -> 99.4 us (level)
  no operation moved by 1% of the time
where the time goes in v5:
time: 99.4 us; the launch traced here: 99.2 us
  Pallas kernels  98.6 us (99%)
    pallas_call x1, Pallas kernels, shards(): pl.pallas_call(step_kernel, out_shape=(jax.ShapeDtypeStruct((4, 8, 32, 12...  96.2 us
    pallas_call x1, Pallas kernels, shards(): pl.pallas_call(finish_kernel, out_shape=(jax.ShapeDtypeStruct((4, 8, 32,...  2.43 us

profile of v5, /device:TPU:1, one launch (start us, length us, event | category | flops | bytes accessed | tf_op | source)
XLA Modules:
  0.0 99.2 jit_solution(14438069078379016472)
XLA Ops:
  0.6 96.2 %shard_map.131 = (bf16[4,8,32,128]{3,2,1,0:T(8,128)(2,1)}, bf16[2,16,112,128]{3,2,1,0:T(8,128)(2,1)}, f32[8,128]{1,0:T(8,128)}) custom-call(bf16[4,8,32,128]{3,2,1,0:T(8,128)(2,1)} %bitcast.16, f32[1,128]{1,0:T(1,128)} %bitcast.20, bf16[27,128,128]{2,1,0:T(8,128)(2,1)} %bitcast.14, f32[1,128]{1,0:T(1,128)} %bitcast.21, bf16[3,128]{1,0:T(4,128)(2,1)} %bitcast.19, ...), custom_call_target="tpu_custom_call" | custom-call | tf_op jit(solution)/shard_map/pallas_call | solution.py:740
  96.8 2.4 %shard_map.132 = (bf16[4,8,32,128]{3,2,1,0:T(8,128)(2,1)}, f32[2,1728,128]{2,1,0:T(8,128)}) custom-call(bf16[4,8,32,128]{3,2,1,0:T(8,128)(2,1)} %get-tuple-element.7.grad_ref, bf16[2,16,112,128]{3,2,1,0:T(8,128)(2,1)} %get-tuple-element.8.summed_ref, f32[8,128]{1,0:T(8,128)} %get-tuple-element.9.scale_ref), custom_call_target="tpu_custom_call" | custom-call | tf_op jit(solution)/shard_map/pallas_call | solution.py:776

commit v6 on v5

--- a/solution.py
+++ b/solution.py
@@ -207,13 +207,13 @@
     for load in loads:
         load.start()
 
-    def stats_start(turn, first, second, before_nearest=lambda: None):
+    def stats_start(turn, first, second, after_farthest=lambda: None):
         stats[turn, clip_slot, 0:1, :] = first
         stats[turn, clip_slot, 1:2, :] = second
         mine = stats.at[turn, clip_slot]
         for index, peer in enumerate(clip_line):
-            if index == 48:
-                before_nearest()
+            if index == 16:
+                after_farthest()
             push(mine, mine, peer, stat_send.at[turn], stat_recv.at[turn])
 
     def stats_wait(turn):
@@ -686,11 +686,15 @@
         squares.append(squares_of(half, chunk))
     own_copy = pltpu.make_async_copy(half, summed_hbm.at[core], load_sem.at[13])
     own_copy.start()
+    other_copies = []
     for turn, chunk in enumerate(chunks):
         arrived(other_half.at[:, chunk], sum_recv.at[10 + turn])
-    other_copy = pltpu.make_async_copy(other_half, summed_hbm.at[1 - core], load_sem.at[14])
-    other_copy.start()
-    for chunk in chunks:
+        other_copies.append(
+            pltpu.make_async_copy(
+                other_half.at[:, chunk], summed_hbm.at[1 - core, :, chunk], load_sem.at[14 + turn]
+            )
+        )
+        other_copies[-1].start()
         squares.append(squares_of(other_half, chunk))
     total = (squares[0] + squares[1]) + (squares[2] + squares[3])
     mean = jnp.sum(total, keepdims=True) / (3456.0 * 128.0)
@@ -716,7 +720,7 @@
         def _():
             arrived(z_in.at[pl.ds(0, 2 * count)], sum_send.at[4 + turn])
 
-    for copy in (out_copy, own_copy, other_copy):
+    for copy in [out_copy, own_copy] + other_copies:
         copy.wait()
 
 
@@ -757,7 +761,7 @@
             wide(3520, 128), wide(3520, 128), wide(9, 128, 128), wide(3520, 128), low(16, 112, 128), low(16, 112, 128), low(16, 112, 128), low(16, 112, 128),
             low(7, 16, 128), low(16, 16, 128), low(7, 16, 128), low(2, 16, 112, 128),
             wide(3, 64, 2, 128), wide(16, 2, 128), wide(4, 2, 128),
-            dma((15,)), dma((5,)), dma((5,)), dma((2, 7)), dma((2, 7)), dma((12,)), dma((12,)),
+            dma((16,)), dma((5,)), dma((5,)), dma((2, 7)), dma((2, 7)), dma((12,)), dma((12,)),
         ],
         compiler_params=pltpu.CompilerParams(
             collective_id=1, has_side_effects=True, vmem_limit_bytes=64 * 1024 * 1024

time: 99.4 us -> 99.7 us (level)
  no operation moved by 1% of the time
where the time goes in v6:
time: 99.7 us; the launch traced here: 99.5 us
  Pallas kernels  98.9 us (99%)
    pallas_call x1, Pallas kernels, shards(): pl.pallas_call(step_kernel, out_shape=(jax.ShapeDtypeStruct((4, 8, 32, 12...  96.4 us
    pallas_call x1, Pallas kernels, shards(): pl.pallas_call(finish_kernel, out_shape=(jax.ShapeDtypeStruct((4, 8, 32,...  2.43 us

profile of v6, /device:TPU:1, one launch (start us, length us, event | category | flops | bytes accessed | tf_op | source)
XLA Modules:
  0.0 99.5 jit_solution(9427388344544930117)
XLA Ops:
  0.6 96.4 %shard_map.131 = (bf16[4,8,32,128]{3,2,1,0:T(8,128)(2,1)}, bf16[2,16,112,128]{3,2,1,0:T(8,128)(2,1)}, f32[8,128]{1,0:T(8,128)}) custom-call(bf16[4,8,32,128]{3,2,1,0:T(8,128)(2,1)} %bitcast.16, f32[1,128]{1,0:T(1,128)} %bitcast.20, bf16[27,128,128]{2,1,0:T(8,128)(2,1)} %bitcast.14, f32[1,128]{1,0:T(1,128)} %bitcast.21, bf16[3,128]{1,0:T(4,128)(2,1)} %bitcast.19, ...), custom_call_target="tpu_custom_call" | custom-call | tf_op jit(solution)/shard_map/pallas_call | solution.py:744
  97.1 2.4 %shard_map.132 = (bf16[4,8,32,128]{3,2,1,0:T(8,128)(2,1)}, f32[2,1728,128]{2,1,0:T(8,128)}) custom-call(bf16[4,8,32,128]{3,2,1,0:T(8,128)(2,1)} %get-tuple-element.7.grad_ref, bf16[2,16,112,128]{3,2,1,0:T(8,128)(2,1)} %get-tuple-element.8.summed_ref, f32[8,128]{1,0:T(8,128)} %get-tuple-element.9.scale_ref), custom_call_target="tpu_custom_call" | custom-call | tf_op jit(solution)/shard_map/pallas_call | solution.py:780
